TPU v7x, 128 devices: a whole 4x4x4 slice. The times are simulated.
128 devices in a mesh: expert: 8 (over z, core), chan: 16 (over x, y).
Axes of the slice: x: 4, y: 4, z: 4, core: 2. Of those that a mesh axis runs over, the one named last changes fastest.
Arguments:
- x_in: bfloat16 [1024, 16384], P(('expert', 'chan')), may hold values from -6 to 6
- z_in: bfloat16 [1024, 16384], P(('expert', 'chan')), may hold values from -6 to 6
- conv_state: bfloat16 [8, 3, 16384], P('expert', None, 'chan'), may hold values from -6 to 6
- ssm_state: float32 [8, 16, 16384], P('expert', None, 'chan'), may hold values from -6 to 6
- conv_weight: bfloat16 [4, 16384], P(None, 'chan'), may hold values from -3 to 3
- conv_bias: bfloat16 [16384], P('chan'), may hold values from -3 to 3
- proj_x: bfloat16 [16384, 544], P('chan'), may hold values from -0.046875 to 0.046875
- dt_gain: bfloat16 [512], replicated, may hold values from 0.5 to 1.5
- dt_weight: bfloat16 [512, 16384], P(None, 'chan'), may hold values from -0.25 to 0.25
- dt_bias: float32 [16384], P('chan'), may hold values from -5 to -1
- a_log: float32 [16, 16384], P(None, 'chan'), may hold values from 0 to 2.5
- skip_scale: float32 [16384], P('chan'), may hold values from 0.5 to 1.5
- out_weight: bfloat16 [16384, 8192], P('chan', 'expert'), may hold values from -0.046875 to 0.046875
- hidden: bfloat16 [1024, 8192], P(('expert', 'chan')), may hold values from -6 to 6
- moe_gain: bfloat16 [8192], replicated, may hold values from 0.5 to 1.5
- router: bfloat16 [8192, 4], replicated, may hold values from -0.125 to 0.125
- routes: int32 [1024, 2], P(('expert', 'chan')), may hold values from 0 to 3, all different within a row; in each aligned block of 8 rows (0 to 7, 8 to 15, ...) at most 5 rows name the same one
- gate_codes: bfloat16 [8, 8192, 6144], P('expert', None, 'chan'), may hold values from 0 to 15, as said below
- gate_zero: int32 [8, 64, 6144], P('expert', None, 'chan'), may hold values from 7 to 8
- gate_scale: bfloat16 [8, 64, 6144], P('expert', None, 'chan'), as said below
- up_codes: bfloat16 [8, 8192, 6144], P('expert', None, 'chan'), may hold values from 0 to 15, as said below
- up_zero: int32 [8, 64, 6144], P('expert', None, 'chan'), may hold values from 7 to 8
- up_scale: bfloat16 [8, 64, 6144], P('expert', None, 'chan'), as said below
- down_codes: bfloat16 [8, 6144, 8192], P('expert', 'chan'), may hold values from 0 to 15, as said below
- down_zero: int32 [8, 48, 8192], P('expert', 'chan'), may hold values from 7 to 8
- down_scale: bfloat16 [8, 48, 8192], P('expert', 'chan'), as said below
Outputs:
- layer_out: bfloat16 [1024, 8192], P(('expert', 'chan'))
- final_state: float32 [8, 16, 16384], P('expert', None, 'chan')
Inputs may be any that keep to these rules, and one draw needn't show every extreme that they name: `routes`: in the rows of one device each expert is named by at most 5 rows, a bound that some block reaches. `gate_codes`: whole numbers. `up_codes`: whole numbers. `down_codes`: whole numbers. `gate_scale`: Positive. `up_scale`: Positive. `down_scale`: Positive.
All inputs are finite; a program needn't handle non-finite values.
Results may differ from a plain program's by a relative error of at most 0.04.
Values may be sent and summed in bfloat16 or wider, within the bound.
No kernel may reach another device: no remote copies, remote signals or barrier semaphores. Data moves between devices by JAX's collectives and lax.ppermute only.
A program may use at most 192 MiB of HBM per device.

v0:
```python
import jax
import jax.numpy as jnp
from jax import lax
from jax.sharding import PartitionSpec as P

epsilon = 1e-05


def dequant(code_tab, zero_tab, scale_tab):
    groups = zero_tab.shape[0]
    shaped = code_tab.astype(jnp.float32).reshape(
        groups, code_tab.shape[0] // groups, code_tab.shape[1]
    )
    dequant_vals = (shaped - zero_tab.astype(jnp.float32)[:, None, :]) * scale_tab.astype(
        jnp.float32
    )[:, None, :]
    return dequant_vals.reshape(code_tab.shape).astype(jnp.bfloat16)


def body(
    x_in,
    z_in,
    conv_state,
    ssm_state,
    conv_weight,
    conv_bias,
    proj_x,
    dt_gain,
    dt_weight,
    dt_bias,
    a_log,
    skip_scale,
    out_weight,
    hidden,
    moe_gain,
    router,
    routes,
    gate_codes,
    gate_zero,
    gate_scale,
    up_codes,
    up_zero,
    up_scale,
    down_codes,
    down_zero,
    down_scale,
):
    owners = lax.axis_size("expert")
    tok_rows = x_in.shape[0]
    model_width = hidden.shape[1]
    x_shard, z_shard = (
        lax.all_to_all(x_in, "chan", split_axis=1, concat_axis=0, tiled=True),
        lax.all_to_all(z_in, "chan", split_axis=1, concat_axis=0, tiled=True),
    )
    seq_len = x_shard.shape[0]
    kernel = conv_weight.shape[0]
    extended = jnp.concatenate([conv_state[0], x_shard], axis=0).astype(jnp.float32)
    conv_pre = jnp.broadcast_to(conv_bias.astype(jnp.float32), x_shard.shape)
    for shift_pos in range(kernel):
        conv_pre = conv_pre + extended[shift_pos : shift_pos + seq_len] * conv_weight[
            shift_pos
        ].astype(jnp.float32)
    u_act = jax.nn.silu(conv_pre).astype(jnp.bfloat16)
    projected = lax.psum(
        jnp.dot(u_act, proj_x, preferred_element_type=jnp.float32).astype(jnp.bfloat16), "chan"
    ).astype(jnp.float32)
    low_rank = dt_weight.shape[0]
    states = a_log.shape[0]
    dt_low = projected[:, :low_rank]
    b_mat = projected[:, low_rank : low_rank + states]
    c_mat = projected[:, low_rank + states :]
    dt_norm = (
        dt_low
        * lax.rsqrt(jnp.mean(dt_low * dt_low, axis=1, keepdims=True) + epsilon)
        * dt_gain.astype(jnp.float32)
    ).astype(jnp.bfloat16)
    step_size = jax.nn.softplus(
        jnp.dot(dt_norm, dt_weight, preferred_element_type=jnp.float32) + dt_bias
    )
    decay_rates = -jnp.exp(a_log)
    u_float = u_act.astype(jnp.float32)
    block_len = 16
    blocks = seq_len // block_len
    inputs = (
        step_size.reshape(blocks, block_len, -1),
        (step_size * u_float).reshape(blocks, block_len, -1),
        b_mat.reshape(blocks, block_len, states),
        c_mat.reshape(blocks, block_len, states),
    )

    def block_step(carried, block_in):
        d_blk, du_blk, b_blk, c_blk = block_in
        outputs = []
        for offset in range(block_len):
            carried = (
                jnp.exp(d_blk[offset][None, :] * decay_rates) * carried
                + b_blk[offset][:, None] * du_blk[offset][None, :]
            )
            outputs.append(jnp.sum(c_blk[offset][:, None] * carried, axis=0))
        return (carried, jnp.stack(outputs))

    final_state, scanned = lax.scan(block_step, ssm_state[0], inputs)
    scan_out = scanned.reshape(seq_len, -1)
    y_out = ((scan_out + skip_scale * u_float) * jax.nn.silu(z_shard.astype(jnp.float32))).astype(
        jnp.bfloat16
    )
    columns = lax.all_gather(out_weight, "expert", axis=1, tiled=True)
    mixer_out = lax.psum_scatter(
        jnp.dot(
            lax.slice_in_dim(y_out, 0, lax.axis_size("chan") * tok_rows, axis=0),
            columns,
            preferred_element_type=jnp.float32,
        ).astype(jnp.bfloat16),
        "chan",
        scatter_dimension=0,
        tiled=True,
    ).astype(jnp.float32)
    residual = hidden.astype(jnp.float32) + mixer_out
    normed = (
        residual
        * lax.rsqrt(jnp.mean(residual * residual, axis=1, keepdims=True) + epsilon)
        * moe_gain.astype(jnp.float32)
    ).astype(jnp.bfloat16)
    logits = jnp.dot(normed, router, preferred_element_type=jnp.float32)
    weights = jnp.exp(logits)
    router_probs = weights / jnp.sum(weights, axis=1, keepdims=True)
    experts = router.shape[1]
    capacity = min(tok_rows, (2 * tok_rows + experts - 1) // experts + tok_rows // 8)
    chosen = routes.reshape(-1)
    gate_flat = jnp.take_along_axis(router_probs, routes, axis=1).reshape(-1)
    onehot = (chosen[:, None] == jnp.arange(experts, dtype=jnp.int32)[None, :]).astype(jnp.int32)
    earlier = jnp.cumsum(onehot, axis=0) - onehot
    slot_index = jnp.sum(earlier * onehot, axis=1)
    target = chosen * capacity + slot_index
    outgoing = (
        jnp.zeros((experts * capacity, model_width), jnp.bfloat16)
        .at[target]
        .set(jnp.repeat(normed, 2, axis=0))
    )
    by_owner = jnp.repeat(outgoing.reshape(experts, capacity, model_width), 2, axis=0)
    w_gate = dequant(gate_codes[0], gate_zero[0], gate_scale[0])
    w_up = dequant(up_codes[0], up_zero[0], up_scale[0])
    w_down = dequant(down_codes[0], down_zero[0], down_scale[0])
    arrived = lax.all_to_all(by_owner, "expert", split_axis=0, concat_axis=0, tiled=True)
    stacked = lax.all_gather(arrived[None], "chan", axis=0, tiled=True)
    expert_lane_rows = stacked.reshape(-1, model_width)
    gate_pre = jnp.dot(expert_lane_rows, w_gate, preferred_element_type=jnp.float32)
    up_pre = jnp.dot(expert_lane_rows, w_up, preferred_element_type=jnp.float32)
    inner_act = (jax.nn.silu(gate_pre) * up_pre).astype(jnp.bfloat16)
    summed = lax.psum_scatter(
        jnp.dot(inner_act, w_down, preferred_element_type=jnp.float32).astype(jnp.bfloat16),
        "chan",
        scatter_dimension=0,
        tiled=True,
    )
    half_sums = summed.reshape(owners, capacity, model_width)
    returned = lax.all_to_all(half_sums, "expert", split_axis=0, concat_axis=0, tiled=True)
    combined = jnp.sum(
        returned.reshape(experts, 2, capacity, model_width).astype(jnp.float32), axis=1
    ).reshape(experts * capacity, model_width)
    picked = jnp.take(combined, target, axis=0)
    moe_out = jnp.sum((picked * gate_flat[:, None]).reshape(tok_rows, 2, model_width), axis=1)
    layer_out = (residual + moe_out).astype(jnp.bfloat16)
    return (layer_out, final_state[None])


def solution(mesh):
    return jax.shard_map(
        body,
        mesh=mesh,
        in_specs=(
            P(("expert", "chan"), None),
            P(("expert", "chan"), None),
            P("expert", None, "chan"),
            P("expert", None, "chan"),
            P(None, "chan"),
            P("chan"),
            P("chan", None),
            P(),
            P(None, "chan"),
            P("chan"),
            P(None, "chan"),
            P("chan"),
            P("chan", "expert"),
            P(("expert", "chan"), None),
            P(),
            P(),
            P(("expert", "chan"), None),
            P("expert", None, "chan"),
            P("expert", None, "chan"),
            P("expert", None, "chan"),
            P("expert", None, "chan"),
            P("expert", None, "chan"),
            P("expert", None, "chan"),
            P("expert", "chan", None),
            P("expert", "chan", None),
            P("expert", "chan", None),
        ),
        out_specs=(P(("expert", "chan"), None), P("expert", None, "chan")),
        check_vma=False,
    )
```

profile of v0, /device:TPU:1, one launch (start us, length us, event | category | flops | bytes accessed | tf_op | source)
XLA Modules:
  0.0 514.4 jit_solution(11091122512409752846)
XLA Ops:
  8.1 7.7 %all-to-all-start = ((bf16[8,16,1024]{2,0,1:T(8,128)(2,1)}), bf16[8,16,1024]{2,0,1:T(8,128)(2,1)S(1)}, u32[]{:S(2)}, u32[]{:S(2)}) async-start(bf16[8,16,1024]{2,0,1:T(8,128)(2,1)} %bitcast.390), calls=%async_computation | async-start | bytes 524288 | tf_op jit(solution)/shard_map/all_to_all | solution.py:52
  15.8 0.7 convert_element_type.203
  16.5 0.9 slice_convert_fusion.3
  17.4 5.8 %all-to-all-done = bf16[8,16,1024]{2,0,1:T(8,128)(2,1)S(1)} async-done(((bf16[8,16,1024]{2,0,1:T(8,128)(2,1)}), bf16[8,16,1024]{2,0,1:T(8,128)(2,1)S(1)}, u32[]{:S(2)}, u32[]{:S(2)}) %all-to-all-start) | async-done | bytes 262176 | tf_op jit(solution)/shard_map/all_to_all | solution.py:52
  23.2 0.8 maximum_convert_fusion
  24.0 0.3 multiply_convert_fusion
  24.4 1.1 convolution_convert_fusion.2
  25.6 0.5 all-gather.4.cloned.1.call-update
  26.1 3.6 all-to-all-start.1
  29.8 77.9 %all-reduce.5.cloned.1.call-done = bf16[128,544]{0,1:T(8,128)(2,1)} async-done(((bf16[128,544]{0,1:T(8,128)(2,1)}), bf16[128,544]{0,1:T(8,128)(2,1)}) %all-reduce.5.cloned.1.call-update) | async-done | bytes 139280 | tf_op jit(solution)/shard_map/psum | solution.py:64
  107.7 0.7 fusion.62
  108.6 0.9 convert_element_type.207
  109.6 1.9 convert_multiply_fusion.1
  111.6 11.8 %while.12 = (s32[]{:T(128)}, f32[16,1024]{1,0:T(8,128)S(1)}, f32[8,16,1024]{2,1,0:T(8,128)S(1)}, f32[8,16,1024]{2,1,0:T(8,128)S(1)}, f32[16,1024]{1,0:T(8,128)S(...) while((s32[]{:T(128)}, f32[16,1024]{1,0:T(8,128)S(1)}, ...), condition=%wide.region_19.20_spmd, body=%wide.region_2.19_spmd.sunk | while | flops 2342929 | bytes 1744149 | solution.py:102
  111.6 0.2 constant_dynamic-slice_fusion.65
  111.9 0.2 fusion.78
  112.2 0.3 multiply_reduce_fusion.24
  113.1 0.2 constant_dynamic-slice_fusion.65
  113.3 0.2 fusion.78
  113.6 0.3 multiply_reduce_fusion.24
  114.6 0.2 constant_dynamic-slice_fusion.65
  114.8 0.2 fusion.78
  115.1 0.3 multiply_reduce_fusion.24
  116.0 0.2 constant_dynamic-slice_fusion.65
  116.6 0.3 multiply_reduce_fusion.24
  117.5 0.2 constant_dynamic-slice_fusion.65
  118.1 0.3 multiply_reduce_fusion.24
  119.0 0.2 constant_dynamic-slice_fusion.65
  119.5 0.3 multiply_reduce_fusion.24
  120.4 0.2 constant_dynamic-slice_fusion.65
  121.0 0.3 multiply_reduce_fusion.24
  121.9 0.2 constant_dynamic-slice_fusion.65
  122.5 0.3 multiply_reduce_fusion.24
  123.4 1.2 fusion.46
  124.7 9.5 %convolution_convert_fusion.1 = bf16[128,8192]{1,0:T(8,128)(2,1)} fusion(bf16[128,1024]{1,0:T(8,128)(2,1)S(1)} %fusion.46, bf16[1024,8192]{1,0:T(8,128)(2,1)} %all-gather.4.cloned.1.call-done), kind=kOutput, calls=%fused_computation.142 | convolution fusion | flops 2148532224 | bytes 19136512 | tf_op jit(solution)/shard_map/dot_general | solution.py:109
  134.7 0.6 dynamic-slice
  135.9 0.2 select_reduce_fusion
  136.1 87.3 %all-reduce.7.cloned.1.call-done = bf16[128,8192]{1,0:T(8,128)(2,1)} async-done(((bf16[128,8192]{1,0:T(8,128)(2,1)}), bf16[128,8192]{1,0:T(8,128)(2,1)}) %all-reduce.7.cloned.1.call-update) | async-done | bytes 2097168
  223.4 1.1 multiply_reduce_fusion.17
  224.5 1.0 multiply_convert_fusion.1
  225.8 1.1 scatter_custom_fusion
  227.1 21.1 %all_to_all.42 = bf16[8,5,8192]{2,1,0:T(8,128)(2,1)S(1)} all-to-all(bf16[8,5,8192]{2,1,0:T(8,128)(2,1)S(1)} %bitcast.313), channel_id=1, replica_groups=mesh['expert'=8,'chan'=16] {'expert'}, dimensions={0} | all-to-all | bytes 1310720 | tf_op jit(solution)/shard_map/all_to_all | solution.py:144
  248.1 1.3 copy.61
  249.4 0.2 reduce-scatter.4.cloned.1.call-start
  249.7 1.1 convert_element_type.239
  250.9 7.5 %fusion.33 = bf16[384,8192]{1,0:T(8,128)(2,1)} fusion(bf16[1,384,8192]{2,1,0:T(8,128)(2,1)} %param.51, f32[3,8192]{1,0:T(4,128)S(1)} %bitcast_convert_fusion, f32[3,8192]{1,0:T(4,128)S(1)} %bitcast.365), kind=kLoop, calls=%fused_computation.135 | loop fusion | flops 12582912 | bytes 12779520 | tf_op jit(solution)/shard_map/convert_element_type | solution.py:17
  258.5 5.3 %fusion.37 = bf16[64,128,384]{2,1,0:T(8,128)(2,1)} fusion(bf16[64,128,384]{2,1,0:T(8,128)(2,1)S(1)} %bitcast.308, f32[64,384]{1,0:T(8,128)S(1)} %bitcast_convert_fusion.2, f32[64,384]{1,0:T(8,128)S(1)} %convert_bitcast_fusion.1), kind=kLoop, calls=%fused_computation.141 | loop fusion | flops 12582912 | bytes 12779520 | tf_op jit(solution)/shard_map/convert_element_type | solution.py:17
  263.8 5.5 %fusion.35 = bf16[64,128,384]{2,1,0:T(8,128)(2,1)} fusion(bf16[64,128,384]{2,1,0:T(8,128)(2,1)S(1)} %bitcast.311, f32[64,384]{1,0:T(8,128)S(1)} %bitcast_convert_fusion.1, f32[64,384]{1,0:T(8,128)S(1)} %convert_bitcast_fusion), kind=kLoop, calls=%fused_computation.138 | loop fusion | flops 12582912 | bytes 12779520 | tf_op jit(solution)/shard_map/convert_element_type | solution.py:17
  269.3 58.3 %all-gather.6.cloned.1.call-done = bf16[128,5,8192]{2,0,1:T(8,128)(2,1)} async-done(((bf16[8,5,8192]{2,0,1:T(8,128)(2,1)}), bf16[128,5,8192]{2,0,1:T(8,128)(2,1)}) %all-gather.6.cloned.1.call-update) | async-done | bytes 10485776 | tf_op jit(solution)/shard_map/all_gather | solution.py:145
  327.6 15.3 %copy.62 = bf16[128,5,8192]{2,1,0:T(8,128)(2,1)} copy(bf16[128,5,8192]{2,0,1:T(8,128)(2,1)} %all-gather.6.cloned.1.call-done) | data formatting | bytes 20971520 | tf_op jit(solution)/shard_map/all_gather | solution.py:145
  342.9 17.0 %reshape.402 = bf16[640,8192]{1,0:T(8,128)(2,1)} reshape(bf16[128,5,8192]{2,1,0:T(8,128)(2,1)} %copy.62) | data formatting | bytes 20971520 | tf_op jit(solution)/shard_map/reshape | solution.py:146
  359.9 10.1 %fusion.64 = f32[640,384]{1,0:T(8,128)S(1)} fusion(bf16[640,8192]{1,0:T(8,128)(2,1)} %reshape.402, bf16[8192,384]{1,0:T(8,128)(2,1)} %bitcast.312), kind=kOutput, calls=%fused_computation.218 | convolution fusion | flops 4026531840 | bytes 17760256 | tf_op jit(solution)/shard_map/dot_general | solution.py:147
  370.0 19.8 %convolution_convert_fusion = bf16[640,8192]{1,0:T(8,128)(2,1)} fusion(bf16[384,8192]{1,0:T(8,128)(2,1)} %fusion.33, bf16[640,8192]{1,0:T(8,128)(2,1)} %reshape.402, bf16[8192,384]{1,0:T(8,128)(2,1)} %bitcast.303, f32[640,384]{1,0:T(8,128)S(1)} %fusion.64), kind=kOutput, calls=%fused_computation.132 | convolution fusion | flops 8059781120 | bytes 34537472 | tf_op jit(solution)/shard_map/dot_general | solution.py:151
  390.2 88.4 %reduce-scatter.4.cloned.1.call-done = bf16[40,8192]{1,0:T(8,128)(2,1)} async-done(((bf16[640,8192]{1,0:T(8,128)(2,1)}), bf16[40,8192]{1,0:T(8,128)(2,1)}) %reduce-scatter.4.cloned.1.call-update) | async-done | bytes 655376
  478.6 2.4 reshape.403
  481.0 6.0 %all-to-all-start.3 = ((bf16[8,5,8192]{2,1,0:T(8,128)(2,1)}), bf16[8,5,8192]{2,1,0:T(8,128)(2,1)}, u32[]{:S(2)}, u32[]{:S(2)}) async-start(bf16[8,5,8192]{2,1,0:T(8,128)(2,1)} %reshape.403), calls=%async_computation.3 | async-start | bytes 2097152 | tf_op jit(solution)/shard_map/all_to_all | solution.py:157
  487.0 0.2 fusion.63
  487.2 0.7 gather_fusion.1
  488.0 14.2 %all-to-all-done.3 = bf16[8,5,8192]{2,1,0:T(8,128)(2,1)} async-done(((bf16[8,5,8192]{2,1,0:T(8,128)(2,1)}), bf16[8,5,8192]{2,1,0:T(8,128)(2,1)}, u32[]{:S(2)}, u32[]{:S(2)}) %all-to-all-start.3) | async-done | bytes 655392 | tf_op jit(solution)/shard_map/all_to_all | solution.py:157
  502.2 1.6 convert_reduce_fusion
  503.9 0.7 gather_fusion
  504.6 0.3 gather.11
  504.9 0.8 multiply_reduce_fusion.16
  505.7 1.6 add_convert_fusion
  (148 shorter events, 8.5 us)
Async XLA Ops:
  8.0 16.4 %copy-start = (bf16[1024,544]{0,1:T(8,128)(2,1)S(1)}, bf16[1024,544]{0,1:T(8,128)(2,1)}, u32[]{:S(2)}) copy-start(bf16[1024,544]{0,1:T(8,128)(2,1)} %param.34) | copy-start | bytes 3342340
  8.0 103.6 %copy-start.3 = (f32[1,16,1024]{2,1,0:T(8,128)S(1)}, f32[1,16,1024]{2,1,0:T(8,128)}, u32[]{:S(2)}) copy-start(f32[1,16,1024]{2,1,0:T(8,128)} %param.31) | copy-start | bytes 196612
  8.0 21.7 %copy-start.15 = (bf16[512]{0:T(512)(128)(2,1)S(1)}, bf16[512]{0:T(512)(128)(2,1)}, u32[]{:S(2)}) copy-start(bf16[512]{0:T(512)(128)(2,1)} %param.35) | copy-start | bytes 3076
  8.0 101.6 %copy-start.13 = (f32[1024]{0:T(1024)S(1)}, f32[1024]{0:T(1024)}, u32[]{:S(2)}) copy-start(f32[1024]{0:T(1024)} %param.37) | copy-start | bytes 12292
  8.0 21.7 %copy-start.8 = (f32[16,1024]{1,0:T(8,128)S(1)}, f32[16,1024]{1,0:T(8,128)}, u32[]{:S(2)}) copy-start(f32[16,1024]{1,0:T(8,128)} %param.38) | copy-start | bytes 196612
  8.1 15.2 %all-to-all-start = ((bf16[8,16,1024]{2,0,1:T(8,128)(2,1)}), bf16[8,16,1024]{2,0,1:T(8,128)(2,1)S(1)}, u32[]{:S(2)}, u32[]{:S(2)}) async-start(bf16[8,16,1024]{2,0,1:T(8,128)(2,1)} %bitcast.390), calls=%async_computation | async-start | bytes 524288 | tf_op jit(solution)/shard_map/all_to_all | solution.py:52
  15.8 91.9 %all-reduce.5.cloned.1.call-start = ((), (), s32[]{:S(2)}) async-start(), calls=%async_computation.5 | async-start | bytes 278528 | tf_op jit(solution)/shard_map/psum | solution.py:64
  17.4 94.2 %copy-start.11 = (f32[1,1024]{1,0:T(1,128)}, f32[1,1024]{1,0:T(1,128)S(1)}, u32[]{:S(2)}) copy-start(f32[1,1024]{1,0:T(1,128)S(1)} %get-tuple-element.216) | copy-start | bytes 12292
  25.5 99.2 %all-gather.4.cloned.1.call-start = ((), (), s32[]{:S(2)}) async-start(), calls=%async_computation.6 | async-start | bytes 18874368 | tf_op jit(solution)/shard_map/all_gather | solution.py:107
  26.1 97.3 %all-to-all-start.1 = ((bf16[8,16,1024]{2,0,1:T(8,128)(2,1)}), bf16[8,16,1024]{2,0,1:T(8,128)(2,1)S(1)}, u32[]{:S(2)}, u32[]{:S(2)}) async-start(bf16[8,16,1024]{2,0,1:T(8,128)(2,1)} %bitcast.95), calls=%async_computation.1 | async-start | bytes 524288 | tf_op jit(solution)/shard_map/all_to_all | solution.py:53
  29.7 193.7 %all-reduce.7.cloned.1.call-start = ((), (), s32[]{:S(2)}) async-start(), calls=%async_computation.8 | async-start | bytes 4194304
  111.6 11.8 %copy-start.14 = (f32[1024]{0:T(1024)S(1)}, f32[1024]{0:T(1024)}, u32[]{:S(2)}) copy-start(f32[1024]{0:T(1024)} %param.39) | copy-start | bytes 12292
  123.4 10.8 %copy-start.2 = (f32[16,1024]{1,0:T(8,128)}, f32[16,1024]{1,0:T(8,128)S(1)}, u32[]{:S(2)}) copy-start(f32[16,1024]{1,0:T(8,128)S(1)} %get-tuple-element.46) | copy-start | bytes 196612
  124.6 9.7 %copy-start.12 = (bf16[8192]{0:T(1024)(128)(2,1)S(1)}, bf16[8192]{0:T(1024)(128)(2,1)}, u32[]{:S(2)}) copy-start(bf16[8192]{0:T(1024)(128)(2,1)} %param.42) | copy-start | bytes 49156
  124.6 9.7 %copy-start.16 = (s32[8,2]{0,1:T(2,128)S(1)}, s32[8,2]{0,1:T(2,128)}, u32[]{:S(2)}) copy-start(s32[8,2]{0,1:T(2,128)} %param.44) | copy-start | bytes 196
  124.6 10.1 %copy-start.18 = (u32[128]{0:T(128)S(1)}, u32[128]{0:T(128)}, u32[]{:S(2)}) copy-start(u32[128]{0:T(128)} %constant.106) | copy-start | bytes 1540
  124.6 98.8 %copy-start.4 = (bf16[8,8192]{1,0:T(8,128)(2,1)S(1)}, bf16[8,8192]{1,0:T(8,128)(2,1)}, u32[]{:S(2)}) copy-start(bf16[8,8192]{1,0:T(8,128)(2,1)} %param.41) | copy-start | bytes 393220
  134.2 116.6 %copy-start.7 = (bf16[1,3,8192]{2,1,0:T(4,128)(2,1)S(1)}, bf16[1,3,8192]{2,1,0:T(4,128)(2,1)}, u32[]{:S(2)}) copy-start(bf16[1,3,8192]{2,1,0:T(4,128)(2,1)} %param.53) | copy-start | bytes 147460
  134.2 193.4 %all-gather.6.cloned.1.call-start = ((), (), s32[]{:S(2)}) async-start(), calls=%async_computation.7 | async-start | bytes 11141120 | tf_op jit(solution)/shard_map/all_gather | solution.py:145
  249.4 9.1 %slice-start = ((s8[6291456]{0:T(1024)(128)(4,1)}), s8[2097152]{0:T(1024)(128)(4,1)S(1)}, s32[]{:S(2)}) async-start(s8[6291456]{0:T(1024)(128)(4,1)} %bitcast.306), calls=%async_computation.10 | async-start | bytes 4194304
  249.4 229.2 %reduce-scatter.4.cloned.1.call-start = ((), (), s32[]{:S(2)}) async-start(), calls=%async_computation.9 | async-start | bytes 11141120
  250.9 7.5 %copy-start.9 = (bf16[1,64,384]{2,1,0:T(8,128)(2,1)S(1)}, bf16[1,64,384]{2,1,0:T(8,128)(2,1)}, u32[]{:S(2)}) copy-start(bf16[1,64,384]{2,1,0:T(8,128)(2,1)} %param.47) | copy-start | bytes 147460
  250.9 7.5 %copy-start.10 = (bf16[1,64,384]{2,1,0:T(8,128)(2,1)S(1)}, bf16[1,64,384]{2,1,0:T(8,128)(2,1)}, u32[]{:S(2)}) copy-start(bf16[1,64,384]{2,1,0:T(8,128)(2,1)} %param.50) | copy-start | bytes 147460
  250.9 7.5 %copy-start.5 = (s32[1,64,384]{2,1,0:T(8,128)S(1)}, s32[1,64,384]{2,1,0:T(8,128)}, u32[]{:S(2)}) copy-start(s32[1,64,384]{2,1,0:T(8,128)} %param.46) | copy-start | bytes 294916
  250.9 7.6 %copy-start.6 = (s32[1,64,384]{2,1,0:T(8,128)S(1)}, s32[1,64,384]{2,1,0:T(8,128)}, u32[]{:S(2)}) copy-start(s32[1,64,384]{2,1,0:T(8,128)} %param.49) | copy-start | bytes 294916
  250.9 7.6 %slice-start.1 = ((s8[6291456]{0:T(1024)(128)(4,1)}), s8[4194304]{0:T(1024)(128)(4,1)S(1)}, s32[]{:S(2)}) async-start(s8[6291456]{0:T(1024)(128)(4,1)} %bitcast.306), calls=%async_computation.11 | async-start | bytes 8388608
  250.9 12.9 %slice-start.2 = ((s8[6291456]{0:T(1024)(128)(4,1)}), s8[4194304]{0:T(1024)(128)(4,1)S(1)}, s32[]{:S(2)}) async-start(s8[6291456]{0:T(1024)(128)(4,1)} %bitcast.309), calls=%async_computation.12 | async-start | bytes 8388608
  258.4 5.3 %slice-start.3 = ((s8[6291456]{0:T(1024)(128)(4,1)}), s8[2097152]{0:T(1024)(128)(4,1)S(1)}, s32[]{:S(2)}) async-start(s8[6291456]{0:T(1024)(128)(4,1)} %bitcast.309), calls=%async_computation.13 | async-start | bytes 4194304
  389.9 97.1 %copy-start.17 = (bf16[8192,4]{0,1:T(4,128)(2,1)S(1)}, bf16[8192,4]{0,1:T(4,128)(2,1)}, u32[]{:S(2)}) copy-start(bf16[8192,4]{0,1:T(4,128)(2,1)} %param.43) | copy-start | bytes 196612
  481.0 21.2 %all-to-all-start.3 = ((bf16[8,5,8192]{2,1,0:T(8,128)(2,1)}), bf16[8,5,8192]{2,1,0:T(8,128)(2,1)}, u32[]{:S(2)}, u32[]{:S(2)}) async-start(bf16[8,5,8192]{2,1,0:T(8,128)(2,1)} %reshape.403), calls=%async_computation.3 | async-start | bytes 2097152 | tf_op jit(solution)/shard_map/all_to_all | solution.py:157
  487.2 20.1 %copy-start.1 = (bf16[1024,544]{0,1:T(8,128)(2,1)S(1)}, bf16[1024,544]{0,1:T(8,128)(2,1)}, u32[]{:S(2)}) copy-start(bf16[1024,544]{0,1:T(8,128)(2,1)} %param.34) | copy-start | bytes 3342340
Sparse Core Ops, SparseCore 0:
  25.6 82.0 all-reduce.4
  134.3 89.0 all-reduce.6
  249.5 78.0 all-gather.5
  390.0 88.5 reduce-scatter.3
Sparse Core Ops, SparseCore 1:
  27.7 85.7 all-gather.3
where the time goes:
time: 516 us; the launch traced here: 514 us
  waiting for transfers between devices  333 us (65%)
  local copies, waits for them, and re-layouts  46 us (9%)
  matrix products  42.7 us (8%)
  other arithmetic  37.6 us (7%)
  blocking collectives  21.1 us (4%)
  starting transfers between devices  17.7 us (3%)
  between operations  16.4 us (3%)
    unnamed x7, waiting for transfers between devices  176 us
    psum x1, waiting for transfers between devices, body(): lax.psum(jnp.dot(u_act, proj_x, preferred_element_type=jnp.float32).astyp...  77.9 us
    all_gather x1, waiting for transfers between devices, body(): stacked = lax.all_gather(arrived[None], 'chan', axis=0, tiled=True)  58.3 us
    all_to_all x1, blocking collectives, body(): lax.all_to_all(by_owner, 'expert', split_axis=0, concat_axis=0, tiled=True)  21.1 us
    dot_general x1, matrix products, body(): jnp.dot(inner_act, w_down, preferred_element_type=jnp.float32)  19.8 us
    convert_element_type x3, other arithmetic, dequant(): return dequant_vals.reshape(code_tab.shape).astype(jnp.bfloat16)  18.2 us
    reshape x1, local copies, waits for them, and re-layouts, body(): expert_lane_rows = stacked.reshape(-1, model_width)  17 us
    all_gather x1, local copies, waits for them, and re-layouts, body(): stacked = lax.all_gather(arrived[None], 'chan', axis=0, tiled=True)  15.3 us
  transfers between devices with their start and end apart: 8, of which 6 were waited for; matrix products, arithmetic and copies ran while one was open for 8% of the time, Pallas kernels for 0%

commit v1 on v0

v1 whole, which is shorter than its diff:
```python
import jax
import jax.numpy as jnp
from jax import lax
from jax.experimental import pallas as pl
from jax.experimental.pallas import tpu as pltpu
from jax.sharding import Mesh, PartitionSpec as P

epsilon = 1e-05
f32 = jnp.float32
bf16 = jnp.bfloat16
RING = 4


def hop(value, axis, step):
    size = lax.axis_size(axis)
    return lax.ppermute(value, axis, [(i, (i + step) % size) for i in range(size)])


def pick(value, index, axis):
    return lax.dynamic_index_in_dim(value, index, axis, keepdims=False)


def spread(block, axis):
    behind, ahead = hop(block, axis, 1), hop(block, axis, -1)
    half = block.shape[-1] // 2
    across = jnp.concatenate(
        [hop(behind[..., :half], axis, 1), hop(ahead[..., half:], axis, -1)], axis=-1
    )
    return [block, behind, across, ahead]


def gather_sum(terms, axis, sign):
    total = terms[0].astype(f32)
    arrived = [hop(terms[s].astype(bf16), axis, sign * s) for s in (1, 2, 3)]
    for term in arrived:
        total = total + term.astype(f32)
    return total


def up_dequant_kernel(place, gc, gz, gs, uc, uz, us, gain, out):
    rows = gc.shape[0]
    groups = gz.shape[0]
    size = rows // groups
    width = gc.shape[1]
    half = groups // 2
    for codes, zero, scale, at in ((gc, gz, gs, 0), (uc, uz, us, width)):
        for g in range(groups):
            values = codes[pl.ds(g * size, size), :].astype(f32) - zero[pl.ds(g, 1), :].astype(f32)
            values = values * scale[pl.ds(g, 1), :]
            weight = gain[pl.ds(g * size, size), :]
            for lane in range(width // 128):
                out[g // half, 0, pl.ds((g % half) * size, size), pl.ds(at + lane * 128, 128)] = (
                    values[:, lane * 128 : (lane + 1) * 128] * weight
                ).astype(bf16)


def up_dequant(place, codes_a, zero_a, scale_a, codes_b, zero_b, scale_b, gain):
    model, width = codes_a.shape
    block = model // 8
    groups = zero_a.shape[0] // 8

    def source(dc, d, place):
        return (lax.rem(place[0] - d + RING, RING) * 2 + lax.rem(place[1] + dc, 2), 0)

    code_spec = pl.BlockSpec((block, width), source)
    group_spec = pl.BlockSpec((groups, width), source)
    return pl.pallas_call(
        up_dequant_kernel,
        grid_spec=pltpu.PrefetchScalarGridSpec(
            num_scalar_prefetch=1,
            grid=(2, RING),
            in_specs=[
                code_spec,
                group_spec,
                group_spec,
                code_spec,
                group_spec,
                group_spec,
                pl.BlockSpec((block, 128), source),
            ],
            out_specs=pl.BlockSpec(
                (2, 1, block // 2, 2 * width), lambda dc, d, place: (0, dc, d, 0)
            ),
        ),
        out_shape=jax.ShapeDtypeStruct((2, 2, model // 4, 2 * width), bf16),
        compiler_params=pltpu.CompilerParams(vmem_limit_bytes=32 * 1024 * 1024),
        cost_estimate=pl.CostEstimate(
            flops=8 * model * width, bytes_accessed=10 * model * width, transcendentals=0
        ),
        name="up_dequant",
    )(place, codes_a, zero_a, scale_a, codes_b, zero_b, scale_b, gain)


def down_dequant_kernel(place, codes, zero, scale, out):
    groups = zero.shape[0]
    size = codes.shape[0] // groups
    half = codes.shape[1] // 2
    for g in range(groups):
        rows = pl.ds(g * size, size)
        for part in range(2):
            cols = pl.ds(part * half, half)
            values = codes[rows, cols].astype(f32) - zero[pl.ds(g, 1), cols].astype(f32)
            out[0, part, rows, :] = (values * scale[pl.ds(g, 1), cols]).astype(bf16)


def down_dequant(place, codes, zero, scale):
    rows, model = codes.shape
    block = model // 8
    groups = zero.shape[0]

    def source(dc, d, place):
        return (0, d * 2 + lax.rem(place[1] + dc, 2))

    return pl.pallas_call(
        down_dequant_kernel,
        grid_spec=pltpu.PrefetchScalarGridSpec(
            num_scalar_prefetch=1,
            grid=(2, RING),
            in_specs=[
                pl.BlockSpec((rows, block), source),
                pl.BlockSpec((groups, block), source),
                pl.BlockSpec((groups, block), source),
            ],
            out_specs=pl.BlockSpec(
                (1, 2, rows, block // 2), lambda dc, d, place: (dc, 0, 0, d)
            ),
        ),
        out_shape=jax.ShapeDtypeStruct((2, 2, rows, model // 4), bf16),
        compiler_params=pltpu.CompilerParams(vmem_limit_bytes=32 * 1024 * 1024),
        cost_estimate=pl.CostEstimate(
            flops=3 * model * rows, bytes_accessed=4 * model * rows, transcendentals=0
        ),
        name="down_dequant",
    )(place, codes, zero, scale)


def pre_kernel(*refs, last, model):
    xs, rest = refs[:10], refs[10:]
    w = rest[0]
    if last:
        pre_in, sq_in, out, rows0, rows1, acc, sq = rest[1:]
    else:
        out, sq_out, rows0, rows1, acc, sq = rest[1:]
    k = pl.program_id(0)
    steps = pl.num_programs(0)
    group = xs[0].shape[0]

    @pl.when(k == 0)
    def _():
        acc[...] = jnp.zeros_like(acc)
        sq[...] = jnp.zeros_like(sq)

    for refs5, rows in ((xs[:5], rows0), (xs[5:], rows1)):
        rows[pl.ds(0, group), :] = refs5[0][...]
        rows[pl.ds(group, group), :] = refs5[1][...]

        @pl.when(k < steps // 2)
        def _(refs5=refs5, rows=rows):
            rows[pl.ds(2 * group, group), :] = refs5[3][...]

        @pl.when(k >= steps // 2)
        def _(refs5=refs5, rows=rows):
            rows[pl.ds(2 * group, group), :] = refs5[4][...]

        rows[pl.ds(3 * group, group), :] = refs5[2][...]
    width = acc.shape[1]
    tile = 256
    for n in range(width // tile):
        cols = pl.ds(n * tile, tile)
        acc[:, cols] += jnp.dot(
            rows0[...], w[0, 0, :, cols], preferred_element_type=f32
        ) + jnp.dot(rows1[...], w[0, 1, :, cols], preferred_element_type=f32)
    for r in range(4):
        at = pl.ds(r * group, group)
        total = sq[at, :]
        for rows in (rows0, rows1):
            for j in range(rows.shape[1] // 128):
                v = rows[at, pl.ds(j * 128, 128)].astype(f32)
                total = total + v * v
        sq[at, :] = total

    @pl.when(k == steps - 1)
    def _():
        if last:
            half = width // 2
            for r in range(4):
                at = pl.ds(r * group, group)
                square = jnp.sum(sq_in[at, :] + sq[at, :], axis=1, keepdims=True)
                scale = lax.rsqrt(square / model + epsilon)
                gate = (pre_in[at, :half] + acc[at, :half]) * scale
                up = (pre_in[at, half:] + acc[at, half:]) * scale
                out[at, :] = (jax.nn.silu(gate) * up).astype(bf16)
        else:
            piece = group // 4
            for i in range(4):
                for j in range(4):
                    there = pl.ds((i * 4 + j) * piece, piece)
                    here = pl.ds((j * 4 + i) * piece, piece)
                    out[there, :] = acc[here, :]
                    sq_out[there, :] = sq[here, :]


def pre_product(part, own, other, w_up, carried, model):
    group, depth = own[0].shape
    width = w_up.shape[-1]
    block = 512
    steps = depth // block
    low = steps // 2
    whole = pl.BlockSpec((group, block), lambda k: (0, k))
    first = pl.BlockSpec((group, block), lambda k: (0, jnp.minimum(k, low - 1)))
    second = pl.BlockSpec((group, block), lambda k: (0, jnp.maximum(k - low, 0)))
    five = [whole, whole, whole, first, second]
    last = carried is not None
    rows = 4 * group
    in_specs = five + five + [pl.BlockSpec((1, 2, block, width), lambda k: (part, 0, k, 0))]
    operands = list(own) + list(other) + [w_up]
    if last:
        in_specs += [
            pl.BlockSpec((rows, width), lambda k: (0, 0)),
            pl.BlockSpec((rows, 128), lambda k: (0, 0)),
        ]
        operands += list(carried)
        out_shape = jax.ShapeDtypeStruct((rows, width // 2), bf16)
        out_specs = pl.BlockSpec((rows, width // 2), lambda k: (0, 0))
    else:
        out_shape = (
            jax.ShapeDtypeStruct((rows, width), f32),
            jax.ShapeDtypeStruct((rows, 128), f32),
        )
        out_specs = (
            pl.BlockSpec((rows, width), lambda k: (0, 0)),
            pl.BlockSpec((rows, 128), lambda k: (0, 0)),
        )

    def kernel(*refs):
        pre_kernel(*refs, last=last, model=model)

    return pl.pallas_call(
        kernel,
        grid=(steps,),
        in_specs=in_specs,
        out_specs=out_specs,
        out_shape=out_shape,
        scratch_shapes=[
            pltpu.VMEM((rows, block), bf16),
            pltpu.VMEM((rows, block), bf16),
            pltpu.VMEM((rows, width), f32),
            pltpu.VMEM((rows, 128), f32),
        ],
        compiler_params=pltpu.CompilerParams(vmem_limit_bytes=40 * 1024 * 1024),
        cost_estimate=pl.CostEstimate(
            flops=4 * rows * depth * width,
            bytes_accessed=4 * depth * (width + rows),
            transcendentals=0,
        ),
        name="pre_last" if last else "pre_first",
    )(*operands)


def column_sums(parts):
    row = lax.broadcasted_iota(jnp.int32, parts[0].shape, 0)
    shift = 1
    while len(parts) > 1:
        keep = (row // shift) % 2 == 0
        parts = [
            jnp.where(keep, a, b) + pltpu.roll(jnp.where(keep, b, a), shift, 0)
            for a, b in zip(parts[::2], parts[1::2])
        ]
        shift *= 2
    return parts[0]


def scan_kernel(place, own, got1, got2, got3, u, zin, dt_gain, dt_weight, dt_bias, a_log, skip,
                ssm, y_out, final, step, driven, bc, b_rows, c_rows, scanned):
    seq, low_rank = u.shape[0], dt_weight.shape[0]
    states, chans = a_log.shape

    def projected(cols):
        return (
            own[:, cols]
            + got1[:, cols].astype(f32)
            + got2[:, cols].astype(f32)
            + got3[:, cols].astype(f32)
        )

    low = projected(slice(0, low_rank))
    norm = low * lax.rsqrt(jnp.mean(low * low, axis=1, keepdims=True) + epsilon)
    norm = (norm * dt_gain[...]).astype(bf16)
    bc[...] = jnp.zeros_like(bc)
    bc[:, pl.ds(0, 2 * states)] = projected(slice(low_rank, low_rank + 2 * states))
    turned = bc[...].T
    for t in range(seq):
        b_rows[pl.ds(t * states, states), :] = jnp.broadcast_to(
            turned[:states, t : t + 1], (states, 128)
        )
        c_rows[pl.ds(t * states, states), :] = jnp.broadcast_to(
            turned[states : 2 * states, t : t + 1], (states, 128)
        )
    tile = 256
    for n in range(chans // tile):
        cols = pl.ds(n * tile, tile)
        raw = jnp.dot(norm, dt_weight[:, cols], preferred_element_type=f32) + dt_bias[:, cols]
        size = jnp.maximum(raw, 0.0) + jnp.log1p(jnp.exp(-jnp.abs(raw)))
        step[:, cols] = size
        driven[:, cols] = size * u[:, cols].astype(f32)
    log2e = 1.4426950408889634
    halves = states // 8
    tiles = chans // 128
    wide = 4
    unroll = 8
    for first in range(0, tiles, wide):
        span = range(first, first + wide)
        rate = [
            [jnp.exp(a_log[pl.ds(h * 8, 8), pl.ds(j * 128, 128)]) * (-log2e) for h in range(halves)]
            for j in span
        ]
        start = tuple(
            ssm[pl.ds(h * 8, 8), pl.ds(j * 128, 128)] for j in span for h in range(halves)
        )

        def advance(block, carried, span=span, rate=rate):
            carried = list(carried)
            at_rows = pl.ds(pl.multiple_of(block * unroll, unroll), unroll)
            base = block * (unroll * states)
            parts = [[] for _ in span]
            d_rows = [step[at_rows, pl.ds(j * 128, 128)] for j in span]
            du_rows = [driven[at_rows, pl.ds(j * 128, 128)] for j in span]
            for i in range(unroll):
                at_t = [
                    pl.ds(pl.multiple_of(base + i * states + h * 8, 8), 8) for h in range(halves)
                ]
                b_t = [b_rows[at, :] for at in at_t]
                c_t = [c_rows[at, :] for at in at_t]
                for n in range(len(span)):
                    d = d_rows[n][i : i + 1]
                    du = du_rows[n][i : i + 1]
                    out = None
                    for h in range(halves):
                        at = n * halves + h
                        carried[at] = jnp.exp2(d * rate[n][h]) * carried[at] + b_t[h] * du
                        term = c_t[h] * carried[at]
                        out = term if out is None else out + term
                    parts[n].append(out)
            for n, j in enumerate(span):
                scanned[at_rows, pl.ds(j * 128, 128)] = column_sums(parts[n])
            return tuple(carried)

        end = lax.fori_loop(0, seq // unroll, advance, start)
        for n, j in enumerate(span):
            for h in range(halves):
                final[pl.ds(h * 8, 8), pl.ds(j * 128, 128)] = end[n * halves + h]
    row = lax.broadcasted_iota(jnp.int32, (seq, seq), 0)
    col = lax.broadcasted_iota(jnp.int32, (seq, seq), 1)
    tok = seq // 16
    block, inside = row // tok, row % tok
    source = ((place[0] + block // 4) % 4) * 4 + (place[1] + block % 4) % 4
    turn = jnp.where(source * tok + inside == col, 1.0, 0.0).astype(bf16)
    for n in range(chans // tile):
        cols = pl.ds(n * tile, tile)
        gate = zin[:, cols].astype(f32)
        y = (scanned[:, cols] + skip[:, cols] * u[:, cols].astype(f32)) * jax.nn.silu(gate)
        y_out[:, cols] = jnp.dot(turn, y.astype(bf16), preferred_element_type=f32).astype(bf16)


def scan_mixer(place, own, got, u, zin, dt_gain, dt_weight, dt_bias, a_log, skip, ssm):
    seq, chans = u.shape
    states = a_log.shape[0]
    vmem = pl.BlockSpec(memory_space=pltpu.VMEM)
    return pl.pallas_call(
        scan_kernel,
        in_specs=[pl.BlockSpec(memory_space=pltpu.SMEM)] + [vmem] * 12,
        out_specs=(vmem, vmem),
        out_shape=(
            jax.ShapeDtypeStruct((seq, chans), bf16),
            jax.ShapeDtypeStruct((states, chans), f32),
        ),
        scratch_shapes=[
            pltpu.VMEM((seq, chans), f32),
            pltpu.VMEM((seq, chans), f32),
            pltpu.VMEM((seq, 128), f32),
            pltpu.VMEM((seq * states, 128), f32),
            pltpu.VMEM((seq * states, 128), f32),
            pltpu.VMEM((seq, chans), f32),
        ],
        compiler_params=pltpu.CompilerParams(vmem_limit_bytes=32 * 1024 * 1024),
        cost_estimate=pl.CostEstimate(
            flops=8 * seq * states * chans,
            bytes_accessed=16 * seq * chans,
            transcendentals=seq * states * chans,
        ),
        name="scan_mixer",
    )(place, own, *got, u, zin, dt_gain, dt_weight, dt_bias, a_log, skip, ssm)


def ranks(member):
    tokens = member.shape[-1]
    before = jnp.arange(tokens)[:, None] < jnp.arange(tokens)[None, :]
    return jnp.sum(
        jnp.where(before, member[..., :, None], 0), axis=-2
    )


def conv_project(x_shard, conv_state, conv_weight, conv_bias, proj_x):
    seq_len = x_shard.shape[0]
    kernel = conv_weight.shape[0]
    extended = jnp.concatenate([conv_state[0], x_shard], axis=0).astype(f32)
    conv_pre = jnp.broadcast_to(conv_bias.astype(f32), x_shard.shape)
    for shift_pos in range(kernel):
        conv_pre = conv_pre + extended[shift_pos : shift_pos + seq_len] * conv_weight[
            shift_pos
        ].astype(f32)
    u_act = jax.nn.silu(conv_pre).astype(bf16)
    return u_act, jnp.dot(u_act, proj_x, preferred_element_type=f32)


def body(
    x_in,
    z_in,
    conv_state,
    ssm_state,
    conv_weight,
    conv_bias,
    proj_x,
    dt_gain,
    dt_weight,
    dt_bias,
    a_log,
    skip_scale,
    out_weight,
    hidden,
    moe_gain,
    router,
    routes,
    gate_codes,
    gate_zero,
    gate_scale,
    up_codes,
    up_zero,
    up_scale,
    down_codes,
    down_zero,
    down_scale,
):
    z, core = lax.axis_index("z"), lax.axis_index("core")
    gx, gy = lax.axis_index("x"), lax.axis_index("y")
    tok = x_in.shape[0]
    model = hidden.shape[1]
    experts = router.shape[1]
    cap = min(tok, (2 * tok + experts - 1) // experts + tok // 8)
    cols = model // 8
    half = cols // 2
    inner_cols = x_in.shape[1] // 16

    both = jnp.stack([x_in.reshape(tok, 16, inner_cols), z_in.reshape(tok, 16, inner_cols)])
    both = lax.all_to_all(
        both.transpose(2, 0, 1, 3), ("x", "y"), split_axis=0, concat_axis=0, tiled=True
    )
    x_shard = both[:, 0].reshape(16 * tok, inner_cols)
    z_shard = both[:, 1].reshape(16 * tok, inner_cols)

    u_act, partial = conv_project(x_shard, conv_state, conv_weight, conv_bias, proj_x)
    sent = partial.astype(bf16)
    got = [hop(sent, "y", s) for s in (1, 2, 3)]
    partial = partial + sum(g.astype(f32) for g in got)
    sent = partial.astype(bf16)
    sent, hidden, routes = lax.optimization_barrier((sent, hidden, routes))
    got = [hop(sent, "x", s) for s in (1, 2, 3)]

    hid = hidden.reshape(tok, RING, 2, cols)
    flags = jnp.pad(routes.astype(bf16), ((0, 0), (0, 126)))
    mine = jnp.concatenate([pick(hid, core, 2).reshape(tok, -1), flags], axis=1)
    theirs = jnp.concatenate([pick(hid, 1 - core, 2).reshape(tok, -1), flags], axis=1)
    pair = jnp.stack([mine, hop(theirs, "core", 1)])
    pair_cols = pair[..., : RING * cols].reshape(2, tok, RING, cols)
    pair_flags = pair[..., RING * cols :]
    pieces = [
        jnp.concatenate([pick(pair_cols, (z + d) % RING, 2), pair_flags], axis=-1)
        for d in range(RING)
    ]
    pieces = jnp.stack([pieces[0]] + [hop(pieces[d], "z", d) for d in (1, 2, 3)])
    hid_t = pieces[..., :cols].reshape(8 * tok, cols)
    route_t = pieces[..., cols : cols + 2].astype(jnp.int32)

    d_ids = jnp.arange(RING)
    k_ids = (z + d_ids) % RING
    src_z = (z - d_ids) % RING
    src_core = (core + jnp.arange(2)) % 2
    src_e = src_z[:, None] * 2 + src_core[None, :]
    member = jnp.any(
        route_t[None] == k_ids[:, None, None, None, None], axis=-1
    ).astype(jnp.int32)
    slot = src_e[None, :, :, None] * cap + ranks(member)
    slot = jnp.where(member > 0, slot, -1)
    own = jnp.where(
        src_z[None, :, None, None] == k_ids[:, None, None, None],
        8 * cap + src_core[None, None, :, None] * tok + jnp.arange(tok)[None, None, None, :],
        -1,
    )
    slot, own = slot.reshape(RING, 1, 8 * tok), own.reshape(RING, 1, 8 * tok)
    row_ids = jnp.arange(8 * cap + 2 * tok)[None, :, None]
    select = ((slot == row_ids) | (own == row_ids)).astype(bf16)

    y_rel, final_state = scan_mixer(
        jnp.stack([gx, gy]).astype(jnp.int32),
        partial,
        got,
        u_act,
        z_shard,
        dt_gain.astype(f32)[None],
        dt_weight,
        dt_bias[None],
        a_log,
        skip_scale[None],
        ssm_state[0],
    )

    y_blocks = [y_rel] + [hop(y_rel, "z", d) for d in (1, 2, 3)]
    y_all = jnp.stack([jnp.stack([b, hop(b, "core", 1)]) for b in y_blocks])
    y_all = y_all.reshape(RING, 2, RING, RING, tok, inner_cols)

    place = jnp.stack([z, core]).astype(jnp.int32)
    place, y_all = lax.optimization_barrier((place, y_all))
    gain = jnp.broadcast_to(moe_gain.astype(f32)[:, None], (model, 128))
    w_up = up_dequant(
        place,
        gate_codes[0],
        gate_zero[0],
        gate_scale[0].astype(f32),
        up_codes[0],
        up_zero[0],
        up_scale[0].astype(f32),
        gain,
    )
    w_down = down_dequant(place, down_codes[0], down_zero[0], down_scale[0].astype(f32))

    def project(rows, weight):
        rows = rows.reshape(-1, inner_cols)
        return jnp.dot(rows, weight, preferred_element_type=f32)

    def mixed(part):
        weight = out_weight[:, part * half : (part + 1) * half]
        first, second = ("y", "x") if part == 0 else ("x", "y")
        axis = 3 if part == 0 else 2
        terms = [
            project(lax.index_in_dim(y_all, s, axis, keepdims=False), weight) for s in range(RING)
        ]
        total = gather_sum(terms, first, 1).reshape(8, RING, tok, half)
        total = gather_sum([total[:, s] for s in range(RING)], second, 1)
        return total.reshape(8 * tok, half)

    def dispatched(part):
        residual = hid_t[:, part * half : (part + 1) * half].astype(f32) + mixed(part)
        rows = jnp.dot(
            select.reshape(-1, 8 * tok), residual.astype(bf16), preferred_element_type=f32
        ).astype(bf16).reshape(RING, -1, half)
        arrived = [rows[0]] + [hop(rows[d], "z", d) for d in (1, 2, 3)]
        routed = jnp.concatenate([a[: 8 * cap] for a in arrived], axis=1)
        kept = jnp.stack([a[8 * cap :] for a in arrived])
        return routed, kept

    def gathered(part, routed):
        first, second = ("x", "y") if part == 0 else ("y", "x")
        near = jnp.concatenate(spread(routed, first), axis=0)
        behind, ahead = hop(near, second, 1), hop(near, second, -1)
        split = near.shape[-1] // 2
        groups = [
            near,
            behind,
            ahead,
            hop(behind[:, :split], second, 1),
            hop(ahead[:, split:], second, -1),
        ]
        return groups, [hop(g, "core", 1) for g in groups]

    routed_0, kept_0 = dispatched(0)
    routed_1, kept_1 = dispatched(1)
    own_0, other_0 = gathered(0, routed_0)
    own_1, other_1 = gathered(1, routed_1)
    carried = pre_product(0, own_0, other_0, w_up, None, model)
    inner_act = pre_product(1, own_1, other_1, w_up, carried, model)
    units = inner_act.shape[-1]
    inner_act = inner_act.reshape(RING, RING, 8 * cap, units)

    def expert_sum(part):
        first, second = ("y", "x") if part == 0 else ("x", "y")
        axis = 1 if part == 0 else 0
        terms = []
        for s in range(RING):
            rows = lax.index_in_dim(inner_act, s, axis, keepdims=False).reshape(-1, units)
            away = jnp.dot(rows, w_down[1, part], preferred_element_type=f32).astype(bf16)
            here = jnp.dot(rows, w_down[0, part], preferred_element_type=f32)
            terms.append(here + hop(away, "core", 1).astype(f32))
        total = gather_sum(terms, first, -1).reshape(RING, 8 * cap, -1)
        return gather_sum([total[s] for s in range(RING)], second, -1).astype(bf16)

    sums = jnp.concatenate([expert_sum(0), expert_sum(1)], axis=1).reshape(RING, 2 * cap, -1)
    back = [pick(sums, (z + d) % RING, 0) for d in range(RING)]
    back = jnp.stack([back[0]] + [hop(back[d], "z", d) for d in (1, 2, 3)])
    back = back.reshape(RING, 2, cap, -1)
    back_own = pick(back, core, 1).reshape(RING * cap, -1)
    back_other = hop(pick(back, 1 - core, 1), "core", 1).reshape(RING * cap, -1)

    kept = jnp.concatenate([kept_0, kept_1], axis=-1).reshape(RING, 2, tok, cols)
    res_own = pick(kept, core, 1)
    res_other = hop(pick(kept, 1 - core, 1), "core", 1)

    def ordered(own_part, other_part):
        low = jnp.where(core == 0, own_part, other_part)
        high = jnp.where(core == 0, other_part, own_part)
        return jnp.stack([low, high], axis=1).transpose(2, 0, 1, 3).reshape(tok, model)

    def absolute(value):
        return jnp.stack([pick(value, (z - i) % RING, 0) for i in range(RING)])

    residual = ordered(absolute(res_own), absolute(res_other)).astype(f32)
    normed = (
        residual
        * lax.rsqrt(jnp.mean(residual * residual, axis=1, keepdims=True) + epsilon)
        * moe_gain.astype(f32)
    ).astype(bf16)
    logits = jnp.dot(normed, router, preferred_element_type=f32)
    weights = jnp.exp(logits)
    probs = weights / jnp.sum(weights, axis=1, keepdims=True)
    named = jnp.any(routes[None] == jnp.arange(experts)[:, None, None], axis=-1)
    rank = ranks(named.astype(jnp.int32))
    gates = jnp.where(
        named[:, :, None] & (rank[:, :, None] == jnp.arange(cap)), probs.T[:, :, None], 0.0
    )
    gates = jnp.stack([pick(gates, (z - d) % RING, 0) for d in range(RING)])
    gates = gates.transpose(1, 0, 2).reshape(tok, RING * cap)

    def combined(rows):
        out = jnp.dot(gates, rows.astype(f32), precision=lax.Precision.HIGHEST)
        return out.reshape(tok, 2, RING, half).transpose(2, 0, 1, 3).reshape(RING, tok, cols)

    layer_out = (residual + ordered(combined(back_own), combined(back_other))).astype(bf16)
    return (layer_out, final_state[None])


def solution(mesh):
    fine = Mesh(mesh.devices.reshape(RING, 2, RING, RING), ("z", "core", "x", "y"))
    e, c = ("z", "core"), ("x", "y")
    every = e + c
    return jax.shard_map(
        body,
        mesh=fine,
        in_specs=(
            P(every, None),
            P(every, None),
            P(e, None, c),
            P(e, None, c),
            P(None, c),
            P(c),
            P(c, None),
            P(),
            P(None, c),
            P(c),
            P(None, c),
            P(c),
            P(c, e),
            P(every, None),
            P(),
            P(),
            P(every, None),
            P(e, None, c),
            P(e, None, c),
            P(e, None, c),
            P(e, None, c),
            P(e, None, c),
            P(e, None, c),
            P(e, c, None),
            P(e, c, None),
            P(e, c, None),
        ),
        out_specs=(P(every, None), P(e, None, c)),
        check_vma=False,
    )
```

time: 516 us -> 313 us (0.61)
  waiting for transfers between devices: 333 us -> 93.8 us
  starting transfers between devices: 17.7 us -> 138 us
  Pallas kernels: 0 us -> 33.5 us
  local copies, waits for them, and re-layouts: 46 us -> 15.3 us
  other arithmetic: 37.6 us -> 8.72 us
  matrix products: 42.7 us -> 17.9 us
  blocking collectives: 21.1 us -> 0 us
  between operations: 16.4 us -> 2.5 us
    unnamed x7 -> x0, waiting for transfers between devices: 176 us -> none
    ppermute x0 -> x86, starting transfers between devices: none -> 131 us  [hop(): lax.ppermute(value, axis, [(i, (i + step) % size) for i in range(size)])]
    ppermute x0 -> x86, waiting for transfers between devices: none -> 85.2 us  [hop(): lax.ppermute(value, axis, [(i, (i + step) % size) for i in range(size)])]
    psum x1 -> x0, waiting for transfers between devices: 77.9 us -> none  [body(): lax.psum(jnp.dot(u_act, proj_x, preferred_element_type=jnp.float32).astyp...]
    all_gather x2 -> x0, waiting for transfers between devices: 58.4 us -> none  [the longest x1 58.3 us: body(): stacked = lax.all_gather(arrived[None], 'chan', axis=0, tiled=True)]
    pallas_call x0 -> x5, Pallas kernels: none -> 33.5 us  [the longest x2 17.1 us: pre_product(): pl.pallas_call(kernel, grid=(steps,), in_specs=in_specs, out_specs=out_sp...]
    dot_general x6 -> x30, matrix products: 42.7 us -> 17.9 us  [the longest x8 6.83 us: project(): return jnp.dot(rows, weight, preferred_element_type=f32)]
    convert_element_type x19 -> x15, other arithmetic: 26 us -> 3.11 us  [the longest x1 1.15 us: body(): sent = partial.astype(bf16)]
  transfers between devices with their start and end apart: 8 -> 87, of which waited for: 6 -> 25; matrix products, arithmetic and copies ran while one was open for 8% -> 8% of each run, Pallas kernels for 0% -> 6%
where the time goes in v1:
time: 313 us; the launch traced here: 310 us
  starting transfers between devices  138 us (44%)
  waiting for transfers between devices  93.8 us (30%)
  Pallas kernels  33.5 us (11%)
  matrix products  17.9 us (6%)
  local copies, waits for them, and re-layouts  15.3 us (5%)
  other arithmetic  8.72 us (3%)
    ppermute x86, starting transfers between devices, hop(): lax.ppermute(value, axis, [(i, (i + step) % size) for i in range(size)])  131 us
    ppermute x86, waiting for transfers between devices, hop(): lax.ppermute(value, axis, [(i, (i + step) % size) for i in range(size)])  85.2 us
    pallas_call x2, Pallas kernels, pre_product(): pl.pallas_call(kernel, grid=(steps,), in_specs=in_specs, out_specs=out_sp...  17.1 us
    all_to_all x1, waiting for transfers between devices, body(): lax.all_to_all(both.transpose(2, 0, 1, 3), ('x', 'y'), split_axis=0, conc...  8.58 us
    pallas_call x1, Pallas kernels, up_dequant(): pl.pallas_call(up_dequant_kernel, grid_spec=pltpu.PrefetchScalarGridSpec(...  7.99 us
    all_to_all x1, starting transfers between devices, body(): lax.all_to_all(both.transpose(2, 0, 1, 3), ('x', 'y'), split_axis=0, conc...  7.72 us
    dot_general x8, matrix products, project(): return jnp.dot(rows, weight, preferred_element_type=f32)  6.83 us
    unnamed x98, local copies, waits for them, and re-layouts  6.68 us
  transfers between devices with their start and end apart: 87, of which 25 were waited for; matrix products, arithmetic and copies ran while one was open for 8% of the time, Pallas kernels for 6%

profile of v1, /device:TPU:1, one launch (start us, length us, event | category | flops | bytes accessed | tf_op | source)
XLA Modules:
  0.0 310.0 jit_solution(7737356451093913198)
XLA Ops:
  0.7 2.0 maximum_bitcast_fusion
  2.7 7.7 %all-to-all-start = ((bf16[16,2,8,1024]{3,2,1,0:T(8,128)(2,1)}), bf16[16,2,8,1024]{3,2,1,0:T(8,128)(2,1)S(1)}, u32[]{:S(2)}, u32[]{:S(2)}) async-start(bf16[16,2,8,1024]{3,2,1,0:T(8,128)(2,1)} %maximum_bitcast_fusion), calls=%async_computation | async-start | bytes 1048576 | tf_op jit(solution)/shard_map/all_to_all | solution.py:455
  12.1 8.6 %all-to-all-done = bf16[16,2,8,1024]{3,2,1,0:T(8,128)(2,1)S(1)} async-done(((bf16[16,2,8,1024]{3,2,1,0:T(8,128)(2,1)}), bf16[16,2,8,1024]{3,2,1,0:T(8,128)(2,1)S(1)}, u32[]{:S(2)}, u32[]{:S(2)}) %all-to-all-start) | async-done | bytes 524320 | tf_op jit(solution)/shard_map/all_to_all | solution.py:455
  21.2 1.3 fusion.89
  23.0 1.2 collective-permute-start.1
  24.2 1.4 collective-permute-start.2
  27.8 2.4 collective-permute-done
  32.4 2.2 collective-permute-start.8
  35.5 3.9 %collective-permute-start.3 = (bf16[8,4224]{1,0:T(8,128)(2,1)S(1)}, bf16[8,4224]{1,0:T(8,128)(2,1)S(1)}, u32[]{:S(2)}, u32[]{:S(2)}) collective-permute-start(bf16[8,4224]{1,0:T(8,128)(2,1)S(1)} %get-tuple-element.93), channel_id=1, source_target_pairs={{0,16},{16,0},{1,17},{17,1},{2,18},{18,2},{3,19},{19,3},{4,20},{20... | collective-permute-start | bytes 202760 | tf_op jit(solution)/shard_map/ppermute | solution.py:16
  40.4 1.7 collective-permute-start.4
  42.1 3.3 %collective-permute-start.5 = (bf16[2,8,1152]{2,1,0:T(8,128)(2,1)S(1)}, bf16[2,8,1152]{2,1,0:T(8,128)(2,1)S(1)}, u32[]{:S(2)}, u32[]{:S(2)}) collective-permute-start(bf16[2,8,1152]{2,1,0:T(8,128)(2,1)S(1)} %get-tuple-element.81), channel_id=1, source_target_pairs={{0,64},{32,96},{64,0},{96,32},{1,65},{33,97},{65,1},{97,33},{2,66}... | collective-permute-start | bytes 110600 | tf_op jit(solution)/shard_map/ppermute | solution.py:16
  49.2 2.4 collective-permute-done.9.got3
  51.6 5.2 %scan_mixer.1 = (bf16[128,1024]{1,0:T(8,128)(2,1)S(1)}, f32[16,1024]{1,0:T(8,128)}) custom-call(s32[2]{0:T(128)S(1)} %pad_add_fusion.1.place, f32[128,544]{1,0:T(8,128)S(1)} %get-tuple-element.23.own, bf16[128,544]{1,0:T(8,128)(2,1)S(1)} %collective-permute-done.7.got1, bf16[128,544]{1,0:T(8,128)(2,1)S(1)} %collective-permute-done.8.got2, ...), custom_call_target="tpu_custom_call" | custom-call | flops 16777216 | bytes 2097152 | tf_op jit(solution)/shard_map/scan_mixer/pallas_call | solution.py:369
  58.3 1.6 collective-permute-start.15
  60.3 2.7 collective-permute-start.10
  63.0 2.6 collective-permute-done.11
  65.6 6.7 %collective-permute-start.12 = (bf16[128,1024]{1,0:T(8,128)(2,1)S(1)}, bf16[128,1024]{1,0:T(8,128)(2,1)S(1)}, u32[]{:S(2)}, u32[]{:S(2)}) collective-permute-start(bf16[128,1024]{1,0:T(8,128)(2,1)S(1)} %collective-permute-done.11), channel_id=1, source_target_pairs={{0,16},{16,0},{1,17},{17,1},{2,18},{18,2},{3,19},{19,3},{4,20},{20... | collective-permute-start | bytes 786440 | tf_op jit(solution)/shard_map/ppermute | solution.py:16
  75.0 1.2 copy-done.35
  76.2 1.2 convolution_convert_fusion.13
  78.6 3.3 %collective-permute-start.18 = (bf16[256,512]{1,0:T(8,128)(2,1)}, bf16[256,512]{1,0:T(8,128)(2,1)}, u32[]{:S(2)}, u32[]{:S(2)}) collective-permute-start(bf16[256,512]{1,0:T(8,128)(2,1)} %convolution_convert_fusion.12), channel_id=1, source_target_pairs={{0,2},{1,3},{2,0},{3,1},{4,6},{5,7},{6,4},{7,5},{8,10},{9,11},{10,... | collective-permute-start | bytes 786440 | tf_op jit(solution)/shard_map/ppermute | solution.py:16
  81.9 1.2 convolution_convert_fusion.11
  83.1 12.8 %collective-permute-start.19 = (bf16[256,512]{1,0:T(8,128)(2,1)}, bf16[256,512]{1,0:T(8,128)(2,1)}, u32[]{:S(2)}, u32[]{:S(2)}) collective-permute-start(bf16[256,512]{1,0:T(8,128)(2,1)} %convolution_convert_fusion.11), channel_id=1, source_target_pairs={{0,3},{1,0},{2,1},{3,2},{4,7},{5,4},{6,5},{7,6},{8,11},{9,8},{10,9... | collective-permute-start | bytes 786440 | tf_op jit(solution)/shard_map/ppermute | solution.py:16
  96.3 1.4 collective-permute-start.26
  98.1 2.2 collective-permute-start.27
  100.4 3.2 %down_dequant.1 = bf16[2,2,384,2048]{3,2,1,0:T(8,128)(2,1)S(1)} custom-call(s32[2]{0:T(128)S(1)} %pad_add_fusion.place, bf16[384,8192]{1,0:T(8,128)(2,1)S(1)} %bitcast.274, s32[3,8192]{1,0:T(4,128)S(1)} %bitcast.282, f32[3,8192]{1,0:T(4,128)S(1)} %bitcast_convert_fusion.scale), custom_call_target="tpu_custom_call" | custom-call | flops 9437184 | bytes 12582912 | tf_op jit(solution)/shard_map/down_dequant/pallas_call | solution.py:114
  103.6 2.6 copy-done.2
  107.4 8.0 %up_dequant.1.refs_10_ = bf16[2,2,2048,768]{3,2,1,0:T(8,128)(2,1)} custom-call(s32[2]{0:T(128)S(1)} %pad_add_fusion.place, bf16[8192,384]{1,0:T(8,128)(2,1)S(1)} %bitcast.277, s32[64,384]{1,0:T(8,128)S(1)} %bitcast.284, f32[64,384]{1,0:T(8,128)S(1)} %get-tuple-element.108.gs, bf16[8192,384]{1,0:T(8,128)(2,1)S(1)} %bitcast.280, s32[64,384]{1,0:T(8,128)S(1)} %bitcast.285, ...), custom_call_target="tpu_custom_call" | custom-call | flops 25165824 | bytes 31457280 | tf_op jit(solution)/shard_map/up_dequant/pallas_call | solution.py:67
  116.2 1.5 convert_add_fusion.1
  117.8 1.2 collective-permute-start.20
  119.9 1.6 collective-permute-start.22
  122.5 1.5 collective-permute-start.29
  124.3 2.2 collective-permute-start.31
  127.2 3.1 collective-permute-start.24
  130.6 1.5 collective-permute-start.32
  132.4 2.2 collective-permute-start.34
  134.7 2.7 collective-permute-start.51
  137.9 2.3 collective-permute-start.38
  140.5 2.7 collective-permute-start.52
  143.4 2.6 collective-permute-start.39
  146.2 2.7 collective-permute-start.54
  149.0 9.1 %collective-permute-start.35 = (bf16[4,8,1024]{2,1,0:T(8,128)(2,1)S(1)}, bf16[4,8,1024]{2,1,0:T(8,128)(2,1)S(1)}, u32[]{:S(2)}, u32[]{:S(2)}) collective-permute-start(bf16[4,8,1024]{2,1,0:T(8,128)(2,1)S(1)} %dynamic-slice_bitcast_fusion.4), channel_id=1, source_target_pairs={{0,16},{16,0},{1,17},{17,1},{2,18},{18,2},{3,19},{19,3},{4,20},{20... | collective-permute-start | bytes 196616 | tf_op jit(solution)/shard_map/ppermute | solution.py:16
  158.1 2.8 collective-permute-start.41
  161.9 2.9 collective-permute-start.56
  165.0 10.1 %collective-permute-done.41.refs_2_ = bf16[160,2048]{1,0:T(8,128)(2,1)S(1)} collective-permute-done((bf16[160,2048]{1,0:T(8,128)(2,1)S(1)}, bf16[160,2048]{1,0:T(8,128)(2,1)S(1)}, u32[]{:S(2)}, u32[]{:S(2)}) %collective-permute-start.41) | collective-permute-done | bytes 655392 | tf_op jit(solution)/shard_map/ppermute | solution.py:16
  175.8 3.4 %collective-permute-start.43 = (bf16[160,1024]{1,0:T(8,128)(2,1)}, bf16[160,1024]{1,0:T(8,128)(2,1)}, u32[]{:S(2)}, u32[]{:S(2)}) collective-permute-start(bf16[160,1024]{1,0:T(8,128)(2,1)} %slice.427), channel_id=1, source_target_pairs={{0,12},{4,0},{8,4},{12,8},{1,13},{5,1},{9,5},{13,9},{2,14},{6,2},{... | collective-permute-start | bytes 983048 | tf_op jit(solution)/shard_map/ppermute | solution.py:16
  182.3 3.4 %collective-permute-done.43.refs_4_ = bf16[160,1024]{1,0:T(8,128)(2,1)} collective-permute-done((bf16[160,1024]{1,0:T(8,128)(2,1)}, bf16[160,1024]{1,0:T(8,128)(2,1)}, u32[]{:S(2)}, u32[]{:S(2)}) %collective-permute-start.43) | collective-permute-done | bytes 327712 | tf_op jit(solution)/shard_map/ppermute | solution.py:16
  185.7 1.8 collective-permute-start.44
  191.5 8.4 %pre_first.1 = (f32[640,768]{1,0:T(8,128)S(1)}, f32[640,128]{1,0:T(8,128)S(1)}) custom-call(bf16[160,2048]{1,0:T(8,128)(2,1)S(1)} %pad_maximum_fusion.1.refs_0_, bf16[160,2048]{1,0:T(8,128)(2,1)S(1)} %collective-permute-done.53.refs_1_, bf16[160,2048]{1,0:T(8,128)(2,1)S(1)} %collective-permute-done.54.refs_2_, ...), custom_call_target="tpu_custom_call" | custom-call | flops 4026531840 | bytes 11534336 | tf_op jit(solution)/shard_map/pre_first/pallas_call | solution.py:238
  200.0 8.7 %pre_last.1 = bf16[640,384]{1,0:T(8,128)(2,1)S(1)} custom-call(bf16[160,2048]{1,0:T(8,128)(2,1)S(1)} %pad_maximum_fusion.refs_0_, bf16[160,2048]{1,0:T(8,128)(2,1)S(1)} %collective-permute-done.40.refs_1_, bf16[160,2048]{1,0:T(8,128)(2,1)S(1)} %copy-done.4, bf16[160,1024]{1,0:T(8,128)(2,1)} %collective-permute-done.42.refs_3_, ...), custom_call_target="tpu_custom_call" | custom-call | flops 4026531840 | bytes 11534336 | tf_op jit(solution)/shard_map/pre_last/pallas_call | solution.py:238
  216.0 3.0 collective-permute-start.64
  223.3 3.5 %collective-permute-start.74 = (bf16[160,2048]{1,0:T(8,128)(2,1)S(1)}, bf16[160,2048]{1,0:T(8,128)(2,1)S(1)}, u32[]{:S(2)}, u32[]{:S(2)}) collective-permute-start(bf16[160,2048]{1,0:T(8,128)(2,1)S(1)} %fusion.9), channel_id=1, source_target_pairs={{0,12},{4,0},{8,4},{12,8},{1,13},{5,1},{9,5},{13,9},{2,14},{6,2},{... | collective-permute-start | bytes 1966088 | tf_op jit(solution)/shard_map/ppermute | solution.py:16
  226.8 19.8 %collective-permute-done.64 = bf16[160,2048]{1,0:T(8,128)(2,1)S(1)} collective-permute-done((bf16[160,2048]{1,0:T(8,128)(2,1)S(1)}, bf16[160,2048]{1,0:T(8,128)(2,1)S(1)}, u32[]{:S(2)}, u32[]{:S(2)}) %collective-permute-start.64) | collective-permute-done | bytes 655392 | tf_op jit(solution)/shard_map/ppermute | solution.py:16
  246.6 1.9 collective-permute-start.76
  248.5 2.1 collective-permute-start.78
  252.2 3.5 %collective-permute-start.69 = (bf16[40,2048]{1,0:T(8,128)(2,1)S(1)}, bf16[40,2048]{1,0:T(8,128)(2,1)S(1)}, u32[]{:S(2)}, u32[]{:S(2)}) collective-permute-start(bf16[40,2048]{1,0:T(8,128)(2,1)S(1)} %get-tuple-element.32), channel_id=1, source_target_pairs={{0,12},{4,0},{8,4},{12,8},{1,13},{5,1},{9,5},{13,9},{2,14},{6,2},{... | collective-permute-start | bytes 491528 | tf_op jit(solution)/shard_map/ppermute | solution.py:16
  256.4 6.6 %collective-permute-done.76 = bf16[160,2048]{1,0:T(8,128)(2,1)S(1)} collective-permute-done((bf16[160,2048]{1,0:T(8,128)(2,1)S(1)}, bf16[160,2048]{1,0:T(8,128)(2,1)S(1)}, u32[]{:S(2)}, u32[]{:S(2)}) %collective-permute-start.76) | collective-permute-done | bytes 655392 | tf_op jit(solution)/shard_map/ppermute | solution.py:16
  263.0 17.6 %collective-permute-done.78 = bf16[160,2048]{1,0:T(8,128)(2,1)S(1)} collective-permute-done((bf16[160,2048]{1,0:T(8,128)(2,1)S(1)}, bf16[160,2048]{1,0:T(8,128)(2,1)S(1)}, u32[]{:S(2)}, u32[]{:S(2)}) %collective-permute-start.78) | collective-permute-done | bytes 655392 | tf_op jit(solution)/shard_map/ppermute | solution.py:16
  281.4 3.5 %collective-permute-start.79 = (bf16[40,2048]{1,0:T(8,128)(2,1)S(1)}, bf16[40,2048]{1,0:T(8,128)(2,1)S(1)}, u32[]{:S(2)}, u32[]{:S(2)}) collective-permute-start(bf16[40,2048]{1,0:T(8,128)(2,1)S(1)} %get-tuple-element.35), channel_id=1, source_target_pairs={{0,3},{1,0},{2,1},{3,2},{4,7},{5,4},{6,5},{7,6},{8,11},{9,8},{10,9... | collective-permute-start | bytes 491528 | tf_op jit(solution)/shard_map/ppermute | solution.py:16
  285.9 5.5 %collective-permute-done.79 = bf16[40,2048]{1,0:T(8,128)(2,1)S(1)} collective-permute-done((bf16[40,2048]{1,0:T(8,128)(2,1)S(1)}, bf16[40,2048]{1,0:T(8,128)(2,1)S(1)}, u32[]{:S(2)}, u32[]{:S(2)}) %collective-permute-start.79) | collective-permute-done | bytes 163872 | tf_op jit(solution)/shard_map/ppermute | solution.py:16
  291.4 4.0 %collective-permute-done.81 = bf16[40,2048]{1,0:T(8,128)(2,1)S(1)} collective-permute-done((bf16[40,2048]{1,0:T(8,128)(2,1)S(1)}, bf16[40,2048]{1,0:T(8,128)(2,1)S(1)}, u32[]{:S(2)}, u32[]{:S(2)}) %collective-permute-start.81) | collective-permute-done | bytes 163872 | tf_op jit(solution)/shard_map/ppermute | solution.py:16
  295.9 2.8 collective-permute-start.83
  299.1 2.1 collective-permute-done.82
  301.2 2.9 collective-permute-done.83
  304.4 2.1 collective-permute-start.85
  (378 shorter events, 54.6 us)
Async XLA Ops:
  2.7 18.0 %all-to-all-start = ((bf16[16,2,8,1024]{3,2,1,0:T(8,128)(2,1)}), bf16[16,2,8,1024]{3,2,1,0:T(8,128)(2,1)S(1)}, u32[]{:S(2)}, u32[]{:S(2)}) async-start(bf16[16,2,8,1024]{3,2,1,0:T(8,128)(2,1)} %maximum_bitcast_fusion), calls=%async_computation | async-start | bytes 1048576 | tf_op jit(solution)/shard_map/all_to_all | solution.py:455
  22.5 7.8 %collective-permute-start = (bf16[128,544]{1,0:T(8,128)(2,1)S(1)}, bf16[128,544]{1,0:T(8,128)(2,1)S(1)}, u32[]{:S(2)}, u32[]{:S(2)}) collective-permute-start(bf16[128,544]{1,0:T(8,128)(2,1)S(1)} %get-tuple-element.95), channel_id=1, source_target_pairs={{0,1},{1,2},{2,3},{3,0},{4,5},{5,6},{6,7},{7,4},{8,9},{9,10},{10,1... | collective-permute-start | bytes 417800 | tf_op jit(solution)/shard_map/ppermute | solution.py:16
  23.0 7.2 %collective-permute-start.1 = (bf16[128,544]{1,0:T(8,128)(2,1)S(1)}, bf16[128,544]{1,0:T(8,128)(2,1)S(1)}, u32[]{:S(2)}, u32[]{:S(2)}) collective-permute-start(bf16[128,544]{1,0:T(8,128)(2,1)S(1)} %get-tuple-element.95), channel_id=1, source_target_pairs={{0,2},{1,3},{2,0},{3,1},{4,6},{5,7},{6,4},{7,5},{8,10},{9,11},{10,... | collective-permute-start | bytes 417800 | tf_op jit(solution)/shard_map/ppermute | solution.py:16
  24.2 6.9 %collective-permute-start.2 = (bf16[128,544]{1,0:T(8,128)(2,1)S(1)}, bf16[128,544]{1,0:T(8,128)(2,1)S(1)}, u32[]{:S(2)}, u32[]{:S(2)}) collective-permute-start(bf16[128,544]{1,0:T(8,128)(2,1)S(1)} %get-tuple-element.95), channel_id=1, source_target_pairs={{0,3},{1,0},{2,1},{3,2},{4,7},{5,4},{6,5},{7,6},{8,11},{9,8},{10,9... | collective-permute-start | bytes 417800 | tf_op jit(solution)/shard_map/ppermute | solution.py:16
  32.3 16.9 %collective-permute-start.7 = (bf16[128,544]{1,0:T(8,128)(2,1)S(1)}, bf16[128,544]{1,0:T(8,128)(2,1)S(1)}, u32[]{:S(2)}, u32[]{:S(2)}) collective-permute-start(bf16[128,544]{1,0:T(8,128)(2,1)S(1)} %get-tuple-element.13), channel_id=1, source_target_pairs={{0,4},{4,8},{8,12},{12,0},{1,5},{5,9},{9,13},{13,1},{2,6},{6,10},{... | collective-permute-start | bytes 417800 | tf_op jit(solution)/shard_map/ppermute | solution.py:16
  32.4 16.8 %collective-permute-start.8 = (bf16[128,544]{1,0:T(8,128)(2,1)S(1)}, bf16[128,544]{1,0:T(8,128)(2,1)S(1)}, u32[]{:S(2)}, u32[]{:S(2)}) collective-permute-start(bf16[128,544]{1,0:T(8,128)(2,1)S(1)} %get-tuple-element.13), channel_id=1, source_target_pairs={{0,8},{4,12},{8,0},{12,4},{1,9},{5,13},{9,1},{13,5},{2,10},{6,14},... | collective-permute-start | bytes 417800 | tf_op jit(solution)/shard_map/ppermute | solution.py:16
  40.4 6.6 %collective-permute-start.4 = (bf16[2,8,1152]{2,1,0:T(8,128)(2,1)S(1)}, bf16[2,8,1152]{2,1,0:T(8,128)(2,1)S(1)}, u32[]{:S(2)}, u32[]{:S(2)}) collective-permute-start(bf16[2,8,1152]{2,1,0:T(8,128)(2,1)S(1)} %get-tuple-element.80), channel_id=1, source_target_pairs={{0,32},{32,64},{64,96},{96,0},{1,33},{33,65},{65,97},{97,1},{2,34}... | collective-permute-start | bytes 110600 | tf_op jit(solution)/shard_map/ppermute | solution.py:16
  42.1 5.7 %collective-permute-start.5 = (bf16[2,8,1152]{2,1,0:T(8,128)(2,1)S(1)}, bf16[2,8,1152]{2,1,0:T(8,128)(2,1)S(1)}, u32[]{:S(2)}, u32[]{:S(2)}) collective-permute-start(bf16[2,8,1152]{2,1,0:T(8,128)(2,1)S(1)} %get-tuple-element.81), channel_id=1, source_target_pairs={{0,64},{32,96},{64,0},{96,32},{1,65},{33,97},{65,1},{97,33},{2,66}... | collective-permute-start | bytes 110600 | tf_op jit(solution)/shard_map/ppermute | solution.py:16
  56.8 8.8 %collective-permute-start.11 = (bf16[128,1024]{1,0:T(8,128)(2,1)S(1)}, bf16[128,1024]{1,0:T(8,128)(2,1)S(1)}, u32[]{:S(2)}, u32[]{:S(2)}) collective-permute-start(bf16[128,1024]{1,0:T(8,128)(2,1)S(1)} %get-tuple-element.14), channel_id=1, source_target_pairs={{0,32},{32,64},{64,96},{96,0},{1,33},{33,65},{65,97},{97,1},{2,34}... | collective-permute-start | bytes 786440 | tf_op jit(solution)/shard_map/ppermute | solution.py:16
  57.6 14.8 %collective-permute-start.13 = (bf16[128,1024]{1,0:T(8,128)(2,1)S(1)}, bf16[128,1024]{1,0:T(8,128)(2,1)S(1)}, u32[]{:S(2)}, u32[]{:S(2)}) collective-permute-start(bf16[128,1024]{1,0:T(8,128)(2,1)S(1)} %get-tuple-element.14), channel_id=1, source_target_pairs={{0,64},{32,96},{64,0},{96,32},{1,65},{33,97},{65,1},{97,33},{2,66}... | collective-permute-start | bytes 786440 | tf_op jit(solution)/shard_map/ppermute | solution.py:16
  58.3 14.0 %collective-permute-start.15 = (bf16[128,1024]{1,0:T(8,128)(2,1)S(1)}, bf16[128,1024]{1,0:T(8,128)(2,1)S(1)}, u32[]{:S(2)}, u32[]{:S(2)}) collective-permute-start(bf16[128,1024]{1,0:T(8,128)(2,1)S(1)} %get-tuple-element.14), channel_id=1, source_target_pairs={{0,96},{32,0},{64,32},{96,64},{1,97},{33,1},{65,33},{97,65},{2,98}... | collective-permute-start | bytes 786440 | tf_op jit(solution)/shard_map/ppermute | solution.py:16
  60.3 12.8 %collective-permute-start.10 = (bf16[128,1024]{1,0:T(8,128)(2,1)S(1)}, bf16[128,1024]{1,0:T(8,128)(2,1)S(1)}, u32[]{:S(2)}, u32[]{:S(2)}) collective-permute-start(bf16[128,1024]{1,0:T(8,128)(2,1)S(1)} %get-tuple-element.14), channel_id=1, source_target_pairs={{0,16},{16,0},{1,17},{17,1},{2,18},{18,2},{3,19},{19,3},{4,20},{20... | collective-permute-start | bytes 786440 | tf_op jit(solution)/shard_map/ppermute | solution.py:16
  65.6 7.9 %collective-permute-start.12 = (bf16[128,1024]{1,0:T(8,128)(2,1)S(1)}, bf16[128,1024]{1,0:T(8,128)(2,1)S(1)}, u32[]{:S(2)}, u32[]{:S(2)}) collective-permute-start(bf16[128,1024]{1,0:T(8,128)(2,1)S(1)} %collective-permute-done.11), channel_id=1, source_target_pairs={{0,16},{16,0},{1,17},{17,1},{2,18},{18,2},{3,19},{19,3},{4,20},{20... | collective-permute-start | bytes 786440 | tf_op jit(solution)/shard_map/ppermute | solution.py:16
  77.3 38.5 %collective-permute-start.17 = (bf16[256,512]{1,0:T(8,128)(2,1)}, bf16[256,512]{1,0:T(8,128)(2,1)S(1)}, u32[]{:S(2)}, u32[]{:S(2)}) collective-permute-start(bf16[256,512]{1,0:T(8,128)(2,1)} %convolution_convert_fusion.13), channel_id=1, source_target_pairs={{0,1},{1,2},{2,3},{3,0},{4,5},{5,6},{6,7},{7,4},{8,9},{9,10},{10,1... | collective-permute-start | bytes 786440 | tf_op jit(solution)/shard_map/ppermute | solution.py:16
  78.6 37.6 %collective-permute-start.18 = (bf16[256,512]{1,0:T(8,128)(2,1)}, bf16[256,512]{1,0:T(8,128)(2,1)}, u32[]{:S(2)}, u32[]{:S(2)}) collective-permute-start(bf16[256,512]{1,0:T(8,128)(2,1)} %convolution_convert_fusion.12), channel_id=1, source_target_pairs={{0,2},{1,3},{2,0},{3,1},{4,6},{5,7},{6,4},{7,5},{8,10},{9,11},{10,... | collective-permute-start | bytes 786440 | tf_op jit(solution)/shard_map/ppermute | solution.py:16
  83.1 33.2 %collective-permute-start.19 = (bf16[256,512]{1,0:T(8,128)(2,1)}, bf16[256,512]{1,0:T(8,128)(2,1)}, u32[]{:S(2)}, u32[]{:S(2)}) collective-permute-start(bf16[256,512]{1,0:T(8,128)(2,1)} %convolution_convert_fusion.11), channel_id=1, source_target_pairs={{0,3},{1,0},{2,1},{3,2},{4,7},{5,4},{6,5},{7,6},{8,11},{9,8},{10,9... | collective-permute-start | bytes 786440 | tf_op jit(solution)/shard_map/ppermute | solution.py:16
  96.3 23.6 %collective-permute-start.26 = (bf16[256,512]{1,0:T(8,128)(2,1)S(1)}, bf16[256,512]{1,0:T(8,128)(2,1)S(1)}, u32[]{:S(2)}, u32[]{:S(2)}) collective-permute-start(bf16[256,512]{1,0:T(8,128)(2,1)S(1)} %convolution_convert_fusion.10), channel_id=1, source_target_pairs={{0,4},{4,8},{8,12},{12,0},{1,5},{5,9},{9,13},{13,1},{2,6},{6,10},{... | collective-permute-start | bytes 786440 | tf_op jit(solution)/shard_map/ppermute | solution.py:16
  98.1 23.4 %collective-permute-start.27 = (bf16[256,512]{1,0:T(8,128)(2,1)S(1)}, bf16[256,512]{1,0:T(8,128)(2,1)S(1)}, u32[]{:S(2)}, u32[]{:S(2)}) collective-permute-start(bf16[256,512]{1,0:T(8,128)(2,1)S(1)} %convolution_convert_fusion.9), channel_id=1, source_target_pairs={{0,8},{4,12},{8,0},{12,4},{1,9},{5,13},{9,1},{13,5},{2,10},{6,14},... | collective-permute-start | bytes 786440 | tf_op jit(solution)/shard_map/ppermute | solution.py:16
  115.8 6.1 %collective-permute-start.28 = (bf16[256,512]{1,0:T(8,128)(2,1)S(1)}, bf16[256,512]{1,0:T(8,128)(2,1)S(1)}, u32[]{:S(2)}, u32[]{:S(2)}) collective-permute-start(bf16[256,512]{1,0:T(8,128)(2,1)S(1)} %convolution_convert_fusion.8), channel_id=1, source_target_pairs={{0,12},{4,0},{8,4},{12,8},{1,13},{5,1},{9,5},{13,9},{2,14},{6,2},{... | collective-permute-start | bytes 786440 | tf_op jit(solution)/shard_map/ppermute | solution.py:16
  117.8 6.5 %collective-permute-start.20 = (bf16[8,8,512]{2,1,0:T(8,128)(2,1)S(1)}, bf16[8,8,512]{2,1,0:T(8,128)(2,1)S(1)}, u32[]{:S(2)}, u32[]{:S(2)}) collective-permute-start(bf16[8,8,512]{2,1,0:T(8,128)(2,1)S(1)} %get-tuple-element.52), channel_id=1, source_target_pairs={{0,4},{4,8},{8,12},{12,0},{1,5},{5,9},{9,13},{13,1},{2,6},{6,10},{... | collective-permute-start | bytes 196616 | tf_op jit(solution)/shard_map/ppermute | solution.py:16
  119.1 7.5 %collective-permute-start.21 = (bf16[8,8,512]{2,1,0:T(8,128)(2,1)S(1)}, bf16[8,8,512]{2,1,0:T(8,128)(2,1)S(1)}, u32[]{:S(2)}, u32[]{:S(2)}) collective-permute-start(bf16[8,8,512]{2,1,0:T(8,128)(2,1)S(1)} %get-tuple-element.54), channel_id=1, source_target_pairs={{0,8},{4,12},{8,0},{12,4},{1,9},{5,13},{9,1},{13,5},{2,10},{6,14},... | collective-permute-start | bytes 196616 | tf_op jit(solution)/shard_map/ppermute | solution.py:16
  119.9 6.6 %collective-permute-start.22 = (bf16[8,8,512]{2,1,0:T(8,128)(2,1)S(1)}, bf16[8,8,512]{2,1,0:T(8,128)(2,1)S(1)}, u32[]{:S(2)}, u32[]{:S(2)}) collective-permute-start(bf16[8,8,512]{2,1,0:T(8,128)(2,1)S(1)} %get-tuple-element.53), channel_id=1, source_target_pairs={{0,12},{4,0},{8,4},{12,8},{1,13},{5,1},{9,5},{13,9},{2,14},{6,2},{... | collective-permute-start | bytes 196616 | tf_op jit(solution)/shard_map/ppermute | solution.py:16
  122.5 7.7 %collective-permute-start.29 = (bf16[8,8,512]{2,1,0:T(8,128)(2,1)S(1)}, bf16[8,8,512]{2,1,0:T(8,128)(2,1)S(1)}, u32[]{:S(2)}, u32[]{:S(2)}) collective-permute-start(bf16[8,8,512]{2,1,0:T(8,128)(2,1)S(1)} %get-tuple-element.55), channel_id=1, source_target_pairs={{0,1},{1,2},{2,3},{3,0},{4,5},{5,6},{6,7},{7,4},{8,9},{9,10},{10,1... | collective-permute-start | bytes 196616 | tf_op jit(solution)/shard_map/ppermute | solution.py:16
  124.0 6.2 %collective-permute-start.30 = (bf16[8,8,512]{2,1,0:T(8,128)(2,1)S(1)}, bf16[8,8,512]{2,1,0:T(8,128)(2,1)S(1)}, u32[]{:S(2)}, u32[]{:S(2)}) collective-permute-start(bf16[8,8,512]{2,1,0:T(8,128)(2,1)S(1)} %get-tuple-element.57), channel_id=1, source_target_pairs={{0,2},{1,3},{2,0},{3,1},{4,6},{5,7},{6,4},{7,5},{8,10},{9,11},{10,... | collective-permute-start | bytes 196616 | tf_op jit(solution)/shard_map/ppermute | solution.py:16
  124.3 5.9 %collective-permute-start.31 = (bf16[8,8,512]{2,1,0:T(8,128)(2,1)S(1)}, bf16[8,8,512]{2,1,0:T(8,128)(2,1)S(1)}, u32[]{:S(2)}, u32[]{:S(2)}) collective-permute-start(bf16[8,8,512]{2,1,0:T(8,128)(2,1)S(1)} %get-tuple-element.56), channel_id=1, source_target_pairs={{0,3},{1,0},{2,1},{3,2},{4,7},{5,4},{6,5},{7,6},{8,11},{9,8},{10,9... | collective-permute-start | bytes 196616 | tf_op jit(solution)/shard_map/ppermute | solution.py:16
  127.2 7.4 %collective-permute-start.24 = (bf16[56,512]{1,0:T(8,128)(2,1)S(1)}, bf16[56,512]{1,0:T(8,128)(2,1)S(1)}, u32[]{:S(2)}, u32[]{:S(2)}) collective-permute-start(bf16[56,512]{1,0:T(8,128)(2,1)S(1)} %get-tuple-element.60), channel_id=1, source_target_pairs={{0,64},{32,96},{64,0},{96,32},{1,65},{33,97},{65,1},{97,33},{2,66}... | collective-permute-start | bytes 172040 | tf_op jit(solution)/shard_map/ppermute | solution.py:16
  130.6 6.8 %collective-permute-start.32 = (bf16[56,512]{1,0:T(8,128)(2,1)S(1)}, bf16[56,512]{1,0:T(8,128)(2,1)S(1)}, u32[]{:S(2)}, u32[]{:S(2)}) collective-permute-start(bf16[56,512]{1,0:T(8,128)(2,1)S(1)} %get-tuple-element.61), channel_id=1, source_target_pairs={{0,32},{32,64},{64,96},{96,0},{1,33},{33,65},{65,97},{97,1},{2,34}... | collective-permute-start | bytes 172040 | tf_op jit(solution)/shard_map/ppermute | solution.py:16
  134.6 5.7 %collective-permute-start.49 = (bf16[40,2048]{1,0:T(8,128)(2,1)S(1)}, bf16[40,2048]{1,0:T(8,128)(2,1)S(1)}, u32[]{:S(2)}, u32[]{:S(2)}) collective-permute-start(bf16[40,2048]{1,0:T(8,128)(2,1)S(1)} %pad_maximum_fusion.4), channel_id=1, source_target_pairs={{0,4},{4,8},{8,12},{12,0},{1,5},{5,9},{9,13},{13,1},{2,6},{6,10},{... | collective-permute-start | bytes 491528 | tf_op jit(solution)/shard_map/ppermute | solution.py:16
  137.5 5.7 %collective-permute-start.36 = (bf16[40,2048]{1,0:T(8,128)(2,1)S(1)}, bf16[40,2048]{1,0:T(8,128)(2,1)S(1)}, u32[]{:S(2)}, u32[]{:S(2)}) collective-permute-start(bf16[40,2048]{1,0:T(8,128)(2,1)S(1)} %pad_maximum_fusion.3), channel_id=1, source_target_pairs={{0,1},{1,2},{2,3},{3,0},{4,5},{5,6},{6,7},{7,4},{8,9},{9,10},{10,1... | collective-permute-start | bytes 491528 | tf_op jit(solution)/shard_map/ppermute | solution.py:16
  146.1 15.5 %collective-permute-start.53 = (bf16[160,2048]{1,0:T(8,128)(2,1)S(1)}, bf16[160,2048]{1,0:T(8,128)(2,1)S(1)}, u32[]{:S(2)}, u32[]{:S(2)}) collective-permute-start(bf16[160,2048]{1,0:T(8,128)(2,1)S(1)} %pad_maximum_fusion.1.refs_0_), channel_id=1, source_target_pairs={{0,1},{1,2},{2,3},{3,0},{4,5},{5,6},{6,7},{7,4},{8,9},{9,10},{10,1... | collective-permute-start | bytes 1966088 | tf_op jit(solution)/shard_map/ppermute | solution.py:16
  146.2 15.7 %collective-permute-start.54 = (bf16[160,2048]{1,0:T(8,128)(2,1)S(1)}, bf16[160,2048]{1,0:T(8,128)(2,1)S(1)}, u32[]{:S(2)}, u32[]{:S(2)}) collective-permute-start(bf16[160,2048]{1,0:T(8,128)(2,1)S(1)} %pad_maximum_fusion.1.refs_0_), channel_id=1, source_target_pairs={{0,3},{1,0},{2,1},{3,2},{4,7},{5,4},{6,5},{7,6},{8,11},{9,8},{10,9... | collective-permute-start | bytes 1966088 | tf_op jit(solution)/shard_map/ppermute | solution.py:16
  148.9 15.9 %collective-permute-start.40 = (bf16[160,2048]{1,0:T(8,128)(2,1)S(1)}, bf16[160,2048]{1,0:T(8,128)(2,1)S(1)}, u32[]{:S(2)}, u32[]{:S(2)}) collective-permute-start(bf16[160,2048]{1,0:T(8,128)(2,1)S(1)} %pad_maximum_fusion.refs_0_), channel_id=1, source_target_pairs={{0,4},{4,8},{8,12},{12,0},{1,5},{5,9},{9,13},{13,1},{2,6},{6,10},{... | collective-permute-start | bytes 1966088 | tf_op jit(solution)/shard_map/ppermute | solution.py:16
  149.0 11.9 %collective-permute-start.35 = (bf16[4,8,1024]{2,1,0:T(8,128)(2,1)S(1)}, bf16[4,8,1024]{2,1,0:T(8,128)(2,1)S(1)}, u32[]{:S(2)}, u32[]{:S(2)}) collective-permute-start(bf16[4,8,1024]{2,1,0:T(8,128)(2,1)S(1)} %dynamic-slice_bitcast_fusion.4), channel_id=1, source_target_pairs={{0,16},{16,0},{1,17},{17,1},{2,18},{18,2},{3,19},{19,3},{4,20},{20... | collective-permute-start | bytes 196616 | tf_op jit(solution)/shard_map/ppermute | solution.py:16
  158.1 16.9 %collective-permute-start.41 = (bf16[160,2048]{1,0:T(8,128)(2,1)S(1)}, bf16[160,2048]{1,0:T(8,128)(2,1)S(1)}, u32[]{:S(2)}, u32[]{:S(2)}) collective-permute-start(bf16[160,2048]{1,0:T(8,128)(2,1)S(1)} %pad_maximum_fusion.refs_0_), channel_id=1, source_target_pairs={{0,12},{4,0},{8,4},{12,8},{1,13},{5,1},{9,5},{13,9},{2,14},{6,2},{... | collective-permute-start | bytes 1966088 | tf_op jit(solution)/shard_map/ppermute | solution.py:16
  161.0 19.8 %collective-permute-start.57 = (bf16[160,2048]{1,0:T(8,128)(2,1)S(1)}, bf16[160,2048]{1,0:T(8,128)(2,1)S(1)}, u32[]{:S(2)}, u32[]{:S(2)}) collective-permute-start(bf16[160,2048]{1,0:T(8,128)(2,1)S(1)} %pad_maximum_fusion.1.refs_0_), channel_id=1, source_target_pairs={{0,16},{16,0},{1,17},{17,1},{2,18},{18,2},{3,19},{19,3},{4,20},{20... | collective-permute-start | bytes 1966088 | tf_op jit(solution)/shard_map/ppermute | solution.py:16
  161.7 17.6 %collective-permute-start.55 = (bf16[160,1024]{1,0:T(8,128)(2,1)S(1)}, bf16[160,1024]{1,0:T(8,128)(2,1)}, u32[]{:S(2)}, u32[]{:S(2)}) collective-permute-start(bf16[160,1024]{1,0:T(8,128)(2,1)S(1)} %slice.434), channel_id=1, source_target_pairs={{0,1},{1,2},{2,3},{3,0},{4,5},{5,6},{6,7},{7,4},{8,9},{9,10},{10,1... | collective-permute-start | bytes 983048 | tf_op jit(solution)/shard_map/ppermute | solution.py:16
  161.9 18.5 %collective-permute-start.56 = (bf16[160,1024]{1,0:T(8,128)(2,1)S(1)}, bf16[160,1024]{1,0:T(8,128)(2,1)}, u32[]{:S(2)}, u32[]{:S(2)}) collective-permute-start(bf16[160,1024]{1,0:T(8,128)(2,1)S(1)} %slice.435), channel_id=1, source_target_pairs={{0,3},{1,0},{2,1},{3,2},{4,7},{5,4},{6,5},{7,6},{8,11},{9,8},{10,9... | collective-permute-start | bytes 983048 | tf_op jit(solution)/shard_map/ppermute | solution.py:16
  164.9 17.3 %collective-permute-start.42 = (bf16[160,1024]{1,0:T(8,128)(2,1)S(1)}, bf16[160,1024]{1,0:T(8,128)(2,1)}, u32[]{:S(2)}, u32[]{:S(2)}) collective-permute-start(bf16[160,1024]{1,0:T(8,128)(2,1)S(1)} %slice.426), channel_id=1, source_target_pairs={{0,4},{4,8},{8,12},{12,0},{1,5},{5,9},{9,13},{13,1},{2,6},{6,10},{... | collective-permute-start | bytes 983048 | tf_op jit(solution)/shard_map/ppermute | solution.py:16
  175.8 9.9 %collective-permute-start.43 = (bf16[160,1024]{1,0:T(8,128)(2,1)}, bf16[160,1024]{1,0:T(8,128)(2,1)}, u32[]{:S(2)}, u32[]{:S(2)}) collective-permute-start(bf16[160,1024]{1,0:T(8,128)(2,1)} %slice.427), channel_id=1, source_target_pairs={{0,12},{4,0},{8,4},{12,8},{1,13},{5,1},{9,5},{13,9},{2,14},{6,2},{... | collective-permute-start | bytes 983048 | tf_op jit(solution)/shard_map/ppermute | solution.py:16
  179.3 8.2 %collective-permute-start.60 = (bf16[160,1024]{1,0:T(8,128)(2,1)}, bf16[160,1024]{1,0:T(8,128)(2,1)}, u32[]{:S(2)}, u32[]{:S(2)}) collective-permute-start(bf16[160,1024]{1,0:T(8,128)(2,1)} %collective-permute-done.55.refs_3_), channel_id=1, source_target_pairs={{0,16},{16,0},{1,17},{17,1},{2,18},{18,2},{3,19},{19,3},{4,20},{20... | collective-permute-start | bytes 983048 | tf_op jit(solution)/shard_map/ppermute | solution.py:16
  180.4 7.1 %collective-permute-start.61 = (bf16[160,1024]{1,0:T(8,128)(2,1)}, bf16[160,1024]{1,0:T(8,128)(2,1)}, u32[]{:S(2)}, u32[]{:S(2)}) collective-permute-start(bf16[160,1024]{1,0:T(8,128)(2,1)} %collective-permute-done.56.refs_4_), channel_id=1, source_target_pairs={{0,16},{16,0},{1,17},{17,1},{2,18},{18,2},{3,19},{19,3},{4,20},{20... | collective-permute-start | bytes 983048 | tf_op jit(solution)/shard_map/ppermute | solution.py:16
  181.7 7.8 %collective-permute-start.58 = (bf16[160,2048]{1,0:T(8,128)(2,1)S(1)}, bf16[160,2048]{1,0:T(8,128)(2,1)}, u32[]{:S(2)}, u32[]{:S(2)}) collective-permute-start(bf16[160,2048]{1,0:T(8,128)(2,1)S(1)} %collective-permute-done.53.refs_1_), channel_id=1, source_target_pairs={{0,16},{16,0},{1,17},{17,1},{2,18},{18,2},{3,19},{19,3},{4,20},{20... | collective-permute-start | bytes 1966088 | tf_op jit(solution)/shard_map/ppermute | solution.py:16
  182.1 7.5 %collective-permute-start.59 = (bf16[160,2048]{1,0:T(8,128)(2,1)S(1)}, bf16[160,2048]{1,0:T(8,128)(2,1)}, u32[]{:S(2)}, u32[]{:S(2)}) collective-permute-start(bf16[160,2048]{1,0:T(8,128)(2,1)S(1)} %collective-permute-done.54.refs_2_), channel_id=1, source_target_pairs={{0,16},{16,0},{1,17},{17,1},{2,18},{18,2},{3,19},{19,3},{4,20},{20... | collective-permute-start | bytes 1966088 | tf_op jit(solution)/shard_map/ppermute | solution.py:16
  185.7 14.2 %collective-permute-start.44 = (bf16[160,2048]{1,0:T(8,128)(2,1)S(1)}, bf16[160,2048]{1,0:T(8,128)(2,1)}, u32[]{:S(2)}, u32[]{:S(2)}) collective-permute-start(bf16[160,2048]{1,0:T(8,128)(2,1)S(1)} %pad_maximum_fusion.refs_0_), channel_id=1, source_target_pairs={{0,16},{16,0},{1,17},{17,1},{2,18},{18,2},{3,19},{19,3},{4,20},{20... | collective-permute-start | bytes 1966088 | tf_op jit(solution)/shard_map/ppermute | solution.py:16
  187.5 12.5 %collective-permute-start.45 = (bf16[160,2048]{1,0:T(8,128)(2,1)S(1)}, bf16[160,2048]{1,0:T(8,128)(2,1)}, u32[]{:S(2)}, u32[]{:S(2)}) collective-permute-start(bf16[160,2048]{1,0:T(8,128)(2,1)S(1)} %collective-permute-done.40.refs_1_), channel_id=1, source_target_pairs={{0,16},{16,0},{1,17},{17,1},{2,18},{18,2},{3,19},{19,3},{4,20},{20... | collective-permute-start | bytes 1966088 | tf_op jit(solution)/shard_map/ppermute | solution.py:16
  187.5 12.5 %collective-permute-start.46 = (bf16[160,2048]{1,0:T(8,128)(2,1)}, bf16[160,2048]{1,0:T(8,128)(2,1)}, u32[]{:S(2)}, u32[]{:S(2)}) collective-permute-start(bf16[160,2048]{1,0:T(8,128)(2,1)} %copy-done.3), channel_id=1, source_target_pairs={{0,16},{16,0},{1,17},{17,1},{2,18},{18,2},{3,19},{19,3},{4,20},{20... | collective-permute-start | bytes 1966088 | tf_op jit(solution)/shard_map/ppermute | solution.py:16
  189.5 10.4 %collective-permute-start.47 = (bf16[160,1024]{1,0:T(8,128)(2,1)}, bf16[160,1024]{1,0:T(8,128)(2,1)S(1)}, u32[]{:S(2)}, u32[]{:S(2)}) collective-permute-start(bf16[160,1024]{1,0:T(8,128)(2,1)} %collective-permute-done.42.refs_3_), channel_id=1, source_target_pairs={{0,16},{16,0},{1,17},{17,1},{2,18},{18,2},{3,19},{19,3},{4,20},{20... | collective-permute-start | bytes 983048 | tf_op jit(solution)/shard_map/ppermute | solution.py:16
  189.6 10.4 %collective-permute-start.48 = (bf16[160,1024]{1,0:T(8,128)(2,1)}, bf16[160,1024]{1,0:T(8,128)(2,1)S(1)}, u32[]{:S(2)}, u32[]{:S(2)}) collective-permute-start(bf16[160,1024]{1,0:T(8,128)(2,1)} %collective-permute-done.43.refs_4_), channel_id=1, source_target_pairs={{0,16},{16,0},{1,17},{17,1},{2,18},{18,2},{3,19},{19,3},{4,20},{20... | collective-permute-start | bytes 983048 | tf_op jit(solution)/shard_map/ppermute | solution.py:16
  213.8 9.6 %collective-permute-start.62 = (bf16[160,2048]{1,0:T(8,128)(2,1)S(1)}, bf16[160,2048]{1,0:T(8,128)(2,1)S(1)}, u32[]{:S(2)}, u32[]{:S(2)}) collective-permute-start(bf16[160,2048]{1,0:T(8,128)(2,1)S(1)} %convolution_convert_fusion.7), channel_id=1, source_target_pairs={{0,16},{16,0},{1,17},{17,1},{2,18},{18,2},{3,19},{19,3},{4,20},{20... | collective-permute-start | bytes 1966088 | tf_op jit(solution)/shard_map/ppermute | solution.py:16
  215.3 6.6 %collective-permute-start.77 = (bf16[160,2048]{1,0:T(8,128)(2,1)S(1)}, bf16[160,2048]{1,0:T(8,128)(2,1)S(1)}, u32[]{:S(2)}, u32[]{:S(2)}) collective-permute-start(bf16[160,2048]{1,0:T(8,128)(2,1)S(1)} %convolution_convert_fusion), channel_id=1, source_target_pairs={{0,16},{16,0},{1,17},{17,1},{2,18},{18,2},{3,19},{19,3},{4,20},{20... | collective-permute-start | bytes 1966088 | tf_op jit(solution)/shard_map/ppermute | solution.py:16
  216.0 30.6 %collective-permute-start.64 = (bf16[160,2048]{1,0:T(8,128)(2,1)S(1)}, bf16[160,2048]{1,0:T(8,128)(2,1)S(1)}, u32[]{:S(2)}, u32[]{:S(2)}) collective-permute-start(bf16[160,2048]{1,0:T(8,128)(2,1)S(1)} %fusion.6), channel_id=1, source_target_pairs={{0,3},{1,0},{2,1},{3,2},{4,7},{5,4},{6,5},{7,6},{8,11},{9,8},{10,9... | collective-permute-start | bytes 1966088 | tf_op jit(solution)/shard_map/ppermute | solution.py:16
  219.5 29.0 %collective-permute-start.66 = (bf16[160,2048]{1,0:T(8,128)(2,1)S(1)}, bf16[160,2048]{1,0:T(8,128)(2,1)S(1)}, u32[]{:S(2)}, u32[]{:S(2)}) collective-permute-start(bf16[160,2048]{1,0:T(8,128)(2,1)S(1)} %fusion.7), channel_id=1, source_target_pairs={{0,2},{1,3},{2,0},{3,1},{4,6},{5,7},{6,4},{7,5},{8,10},{9,11},{10,... | collective-permute-start | bytes 1966088 | tf_op jit(solution)/shard_map/ppermute | solution.py:16
  219.6 31.8 %collective-permute-start.68 = (bf16[160,2048]{1,0:T(8,128)(2,1)S(1)}, bf16[160,2048]{1,0:T(8,128)(2,1)S(1)}, u32[]{:S(2)}, u32[]{:S(2)}) collective-permute-start(bf16[160,2048]{1,0:T(8,128)(2,1)S(1)} %fusion.8), channel_id=1, source_target_pairs={{0,1},{1,2},{2,3},{3,0},{4,5},{5,6},{6,7},{7,4},{8,9},{9,10},{10,1... | collective-permute-start | bytes 1966088 | tf_op jit(solution)/shard_map/ppermute | solution.py:16
  221.8 33.8 %collective-permute-start.72 = (bf16[160,2048]{1,0:T(8,128)(2,1)S(1)}, bf16[160,2048]{1,0:T(8,128)(2,1)S(1)}, u32[]{:S(2)}, u32[]{:S(2)}) collective-permute-start(bf16[160,2048]{1,0:T(8,128)(2,1)S(1)} %convolution_convert_fusion.3), channel_id=1, source_target_pairs={{0,16},{16,0},{1,17},{17,1},{2,18},{18,2},{3,19},{19,3},{4,20},{20... | collective-permute-start | bytes 1966088 | tf_op jit(solution)/shard_map/ppermute | solution.py:16
  223.3 32.3 %collective-permute-start.74 = (bf16[160,2048]{1,0:T(8,128)(2,1)S(1)}, bf16[160,2048]{1,0:T(8,128)(2,1)S(1)}, u32[]{:S(2)}, u32[]{:S(2)}) collective-permute-start(bf16[160,2048]{1,0:T(8,128)(2,1)S(1)} %fusion.9), channel_id=1, source_target_pairs={{0,12},{4,0},{8,4},{12,8},{1,13},{5,1},{9,5},{13,9},{2,14},{6,2},{... | collective-permute-start | bytes 1966088 | tf_op jit(solution)/shard_map/ppermute | solution.py:16
  246.6 16.4 %collective-permute-start.76 = (bf16[160,2048]{1,0:T(8,128)(2,1)S(1)}, bf16[160,2048]{1,0:T(8,128)(2,1)S(1)}, u32[]{:S(2)}, u32[]{:S(2)}) collective-permute-start(bf16[160,2048]{1,0:T(8,128)(2,1)S(1)} %fusion.10), channel_id=1, source_target_pairs={{0,8},{4,12},{8,0},{12,4},{1,9},{5,13},{9,1},{13,5},{2,10},{6,14},... | collective-permute-start | bytes 1966088 | tf_op jit(solution)/shard_map/ppermute | solution.py:16
  248.5 32.0 %collective-permute-start.78 = (bf16[160,2048]{1,0:T(8,128)(2,1)S(1)}, bf16[160,2048]{1,0:T(8,128)(2,1)S(1)}, u32[]{:S(2)}, u32[]{:S(2)}) collective-permute-start(bf16[160,2048]{1,0:T(8,128)(2,1)S(1)} %fusion.11), channel_id=1, source_target_pairs={{0,4},{4,8},{8,12},{12,0},{1,5},{5,9},{9,13},{13,1},{2,6},{6,10},{... | collective-permute-start | bytes 1966088 | tf_op jit(solution)/shard_map/ppermute | solution.py:16
  252.2 32.7 %collective-permute-start.69 = (bf16[40,2048]{1,0:T(8,128)(2,1)S(1)}, bf16[40,2048]{1,0:T(8,128)(2,1)S(1)}, u32[]{:S(2)}, u32[]{:S(2)}) collective-permute-start(bf16[40,2048]{1,0:T(8,128)(2,1)S(1)} %get-tuple-element.32), channel_id=1, source_target_pairs={{0,12},{4,0},{8,4},{12,8},{1,13},{5,1},{9,5},{13,9},{2,14},{6,2},{... | collective-permute-start | bytes 491528 | tf_op jit(solution)/shard_map/ppermute | solution.py:16
  255.7 29.9 %collective-permute-start.70 = (bf16[40,2048]{1,0:T(8,128)(2,1)S(1)}, bf16[40,2048]{1,0:T(8,128)(2,1)S(1)}, u32[]{:S(2)}, u32[]{:S(2)}) collective-permute-start(bf16[40,2048]{1,0:T(8,128)(2,1)S(1)} %get-tuple-element.34), channel_id=1, source_target_pairs={{0,8},{4,12},{8,0},{12,4},{1,9},{5,13},{9,1},{13,5},{2,10},{6,14},... | collective-permute-start | bytes 491528 | tf_op jit(solution)/shard_map/ppermute | solution.py:16
  255.7 30.1 %collective-permute-start.71 = (bf16[40,2048]{1,0:T(8,128)(2,1)S(1)}, bf16[40,2048]{1,0:T(8,128)(2,1)S(1)}, u32[]{:S(2)}, u32[]{:S(2)}) collective-permute-start(bf16[40,2048]{1,0:T(8,128)(2,1)S(1)} %get-tuple-element.33), channel_id=1, source_target_pairs={{0,4},{4,8},{8,12},{12,0},{1,5},{5,9},{9,13},{13,1},{2,6},{6,10},{... | collective-permute-start | bytes 491528 | tf_op jit(solution)/shard_map/ppermute | solution.py:16
  281.4 10.0 %collective-permute-start.79 = (bf16[40,2048]{1,0:T(8,128)(2,1)S(1)}, bf16[40,2048]{1,0:T(8,128)(2,1)S(1)}, u32[]{:S(2)}, u32[]{:S(2)}) collective-permute-start(bf16[40,2048]{1,0:T(8,128)(2,1)S(1)} %get-tuple-element.35), channel_id=1, source_target_pairs={{0,3},{1,0},{2,1},{3,2},{4,7},{5,4},{6,5},{7,6},{8,11},{9,8},{10,9... | collective-permute-start | bytes 491528 | tf_op jit(solution)/shard_map/ppermute | solution.py:16
  284.9 6.5 %collective-permute-start.80 = (bf16[40,2048]{1,0:T(8,128)(2,1)S(1)}, bf16[40,2048]{1,0:T(8,128)(2,1)S(1)}, u32[]{:S(2)}, u32[]{:S(2)}) collective-permute-start(bf16[40,2048]{1,0:T(8,128)(2,1)S(1)} %get-tuple-element.37), channel_id=1, source_target_pairs={{0,2},{1,3},{2,0},{3,1},{4,6},{5,7},{6,4},{7,5},{8,10},{9,11},{10,... | collective-permute-start | bytes 491528 | tf_op jit(solution)/shard_map/ppermute | solution.py:16
  284.9 10.5 %collective-permute-start.81 = (bf16[40,2048]{1,0:T(8,128)(2,1)S(1)}, bf16[40,2048]{1,0:T(8,128)(2,1)S(1)}, u32[]{:S(2)}, u32[]{:S(2)}) collective-permute-start(bf16[40,2048]{1,0:T(8,128)(2,1)S(1)} %get-tuple-element.36), channel_id=1, source_target_pairs={{0,1},{1,2},{2,3},{3,0},{4,5},{5,6},{6,7},{7,4},{8,9},{9,10},{10,1... | collective-permute-start | bytes 491528 | tf_op jit(solution)/shard_map/ppermute | solution.py:16
  295.9 8.2 %collective-permute-start.83 = (bf16[10,4096]{1,0:T(8,128)(2,1)S(1)}, bf16[10,4096]{1,0:T(8,128)(2,1)S(1)}, u32[]{:S(2)}, u32[]{:S(2)}) collective-permute-start(bf16[10,4096]{1,0:T(8,128)(2,1)S(1)} %get-tuple-element.41), channel_id=1, source_target_pairs={{0,64},{32,96},{64,0},{96,32},{1,65},{33,97},{65,1},{97,33},{2,66}... | collective-permute-start | bytes 245768 | tf_op jit(solution)/shard_map/ppermute | solution.py:16
  (69 other events, 638.8 us)
